TPU v7x, 512 devices: a whole 4x4x16 slice. The times are simulated.
512 devices in a mesh: doc: 4 (over y_hi, core), seq: 128 (over z, y_lo, x).
Axes of the slice: x: 4, y: 4 (y_hi: 2, y_lo: 2; y = y_hi * 2 + y_lo), z: 16, core: 2. Of those that a mesh axis runs over, the one named last changes fastest.
Arguments:
- queries: bfloat16 [65536, 512], P(('doc', 'seq')), parts along dimension 0, may hold values from -26 to 26
- key_vectors: bfloat16 [65536, 512], P(('doc', 'seq')), parts along dimension 0, may hold values from -26 to 26
- value_vectors: bfloat16 [65536, 512], P(('doc', 'seq')), parts along dimension 0, may hold values from -6 to 6
- output_grad: bfloat16 [65536, 512], P(('doc', 'seq')), parts along dimension 0, may hold values from -6 to 6
- rand_pick: int32 [1024, 3], P('doc'), parts along dimension 0, may hold values from 0 to 1
- global_ids: int32 [8], P('doc'), parts along dimension 0, may hold values from 0 to 255
Outputs:
- grad_queries: bfloat16 [65536, 512], P(('doc', 'seq')), parts along dimension 0
- grad_keys: bfloat16 [65536, 512], P(('doc', 'seq')), parts along dimension 0
- grad_values: bfloat16 [65536, 512], P(('doc', 'seq')), parts along dimension 0
There are 4 independent parts, one for each index of `doc`. A program takes and returns all parts, laid end to end along the dimension named above; each array names one. Nothing has to cross between parts.
All inputs are finite; a program needn't handle non-finite values.
Results may differ from a plain program's by a relative error of at most 0.012.
Values may be sent and summed in bfloat16 or wider, within the bound.
A program may use at most 64 MiB of HBM per device.

v0:
```python
import math

import jax
import jax.numpy as jnp
from jax import lax
from jax.sharding import PartitionSpec as P

HEADS = 8
BLOCK = 64
RAND = 3
GLOBAL = 2


def extended_2(block, sides, width):
    for axis, dim in sides:
        count = lax.axis_size(axis)
        forward = [(i, i + 1) for i in range(count - 1)]
        backward = [(target, source) for source, target in forward]
        low = lax.ppermute(
            lax.slice_in_dim(block, block.shape[dim] - width, None, axis=dim), axis, forward
        )
        high = lax.ppermute(lax.slice_in_dim(block, 0, width, axis=dim), axis, backward)
        block = jnp.concatenate([low, block, high], axis=dim)
    return block


def shifted(block, axis, distance):
    devices = range(lax.axis_size(axis))
    route = [((i - distance) % len(devices), i) for i in devices]
    return lax.ppermute(block, axis, route)


def broadcast(block, axis, holder):
    block = jnp.where(lax.axis_index(axis) == holder, block, jnp.zeros_like(block))
    return lax.psum(block, axis)


def key_grads(probs_half, grad_half, query_block, grad_block, scale):
    width = query_block.shape[-1]
    head_size = width // HEADS
    query_heads = query_block.reshape(-1, HEADS, head_size)
    grad_heads = grad_block.reshape(-1, HEADS, head_size)
    grad_key = (
        jnp.einsum("hqk,qhe->khe", grad_half, query_heads, preferred_element_type=jnp.float32)
        * scale
    )
    grad_value = jnp.einsum(
        "hqk,qhe->khe", probs_half, grad_heads, preferred_element_type=jnp.float32
    )
    count = grad_key.shape[0]
    return jnp.concatenate(
        [grad_key.reshape(count, width), grad_value.reshape(count, width)], axis=1
    )


def attend(query_block, grad_block, listed, valid, scale):
    width = query_block.shape[-1]
    head_size = width // HEADS
    query_heads = query_block.reshape(-1, HEADS, head_size)
    grad_heads = grad_block.reshape(-1, HEADS, head_size)
    key_heads = listed[:, :width].reshape(-1, HEADS, head_size)
    value_heads = listed[:, width:].reshape(-1, HEADS, head_size)
    scores = (
        jnp.einsum("qhe,khe->hqk", query_heads, key_heads, preferred_element_type=jnp.float32)
        * scale
    )
    scores = jnp.where(valid[None, None, :], scores, -1e30)
    row_max = jnp.max(scores, axis=-1, keepdims=True)
    expo = jnp.exp(scores - row_max)
    row_total = jnp.sum(expo, axis=-1, keepdims=True)
    probs = expo / row_total
    probs_half = probs.astype(jnp.bfloat16)
    attended = jnp.einsum(
        "hqk,khe->qhe", probs_half, value_heads, preferred_element_type=jnp.float32
    )
    row_dot = jnp.sum(grad_heads.astype(jnp.float32) * attended, axis=-1).T
    grad_probs = jnp.einsum(
        "qhe,khe->hqk", grad_heads, value_heads, preferred_element_type=jnp.float32
    )
    grad_scores = probs * (grad_probs - row_dot[:, :, None])
    grad_half = grad_scores.astype(jnp.bfloat16)
    grad_query = (
        jnp.einsum("hqk,khe->qhe", grad_half, key_heads, preferred_element_type=jnp.float32) * scale
    )
    return (probs_half, grad_half, grad_query.reshape(-1, width), row_max, row_total, row_dot)


def on_device(queries, key_vectors, value_vectors, output_grad, rand_pick, global_ids):
    group = lax.axis_size("seq")
    position = lax.axis_index("seq")
    rows, width = queries.shape
    local_blocks = rows // BLOCK
    head_size = width // HEADS
    scale = 1.0 / math.sqrt(head_size)
    all_blocks = local_blocks * group
    near = (3 + GLOBAL) * BLOCK
    pairs = jnp.concatenate([key_vectors, value_vectors], axis=1)
    padded = extended_2(pairs, (("seq", 0),), BLOCK)
    extended = padded.reshape(local_blocks + 2, BLOCK, 2 * width)
    own_pairs = extended[1:-1]
    block_range = jnp.arange(local_blocks, dtype=jnp.int32)
    routes = []
    fetched = []
    for slot_idx in range(RAND):
        distance = (slot_idx + 1) * group // 4
        arrived = None
        for lag in range(2):
            target = (position + distance + lag) % group
            picks = lax.dynamic_slice_in_dim(rand_pick, target * local_blocks, local_blocks, 0)[
                :, slot_idx
            ]
            behind = block_range - picks
            if lag == 0:
                inside = behind >= 0
                local_index = jnp.clip(behind, 0, local_blocks - 1)
            else:
                inside = behind < 0
                local_index = jnp.clip(behind + local_blocks, 0, local_blocks - 1)
            routes.append((slot_idx, distance + lag, inside, local_index))
            outgoing = jnp.where(
                inside[:, None, None],
                jnp.take(own_pairs, local_index, axis=0),
                jnp.zeros((), own_pairs.dtype),
            )
            moved = shifted(outgoing, "seq", distance + lag)
            arrived = moved if arrived is None else arrived + moved
        fetched.append(arrived)
    random_pairs = jnp.stack(fetched, axis=1).reshape(local_blocks, RAND * BLOCK, 2 * width)
    roots = global_ids // local_blocks
    offsets = global_ids % local_blocks
    global_list = []
    for slot_idx in range(GLOBAL):
        picked = lax.dynamic_index_in_dim(own_pairs, offsets[slot_idx], 0, keepdims=False)
        global_list.append(broadcast(picked, "seq", roots[slot_idx]))
    global_pairs = jnp.concatenate(global_list, axis=0)
    segment = jnp.arange((3 + GLOBAL + RAND) * BLOCK) // BLOCK
    query_blocks = queries.reshape(local_blocks, BLOCK, width)
    grad_blocks = output_grad.reshape(local_blocks, BLOCK, width)

    def visit(global_acc, inputs):
        query_block, grad_block, remote_keys, block_idx = inputs
        window = lax.dynamic_slice_in_dim(extended, block_idx, 3, 0).reshape(3 * BLOCK, 2 * width)
        listed = jnp.concatenate([window, global_pairs, remote_keys], axis=0)
        overall = position * local_blocks + block_idx
        valid = ((segment != 0) | (overall > 0)) & ((segment != 2) | (overall < all_blocks - 1))
        probs_half, grad_half, grad_query, row_max, row_total, row_dot = attend(
            query_block, grad_block, listed, valid, scale
        )
        grads = key_grads(probs_half, grad_half, query_block, grad_block, scale)
        extra = grads[near:].reshape(RAND, BLOCK, 2 * width)
        window_part = grads[: 3 * BLOCK].reshape(3, BLOCK, 2 * width)
        global_acc = global_acc + grads[3 * BLOCK : near].reshape(GLOBAL, BLOCK, 2 * width)
        return (global_acc, (grad_query.astype(jnp.bfloat16), window_part, extra))

    start = jnp.zeros((GLOBAL, BLOCK, 2 * width), jnp.float32)
    steps_in = (query_blocks, grad_blocks, random_pairs, block_range)
    global_acc, (grad_query, window_parts, extra) = lax.scan(visit, start, steps_in)
    window_acc = jnp.pad(window_parts[:, 0], ((0, 2), (0, 0), (0, 0)))
    window_acc = window_acc + jnp.pad(window_parts[:, 1], ((1, 1), (0, 0), (0, 0)))
    window_acc = window_acc + jnp.pad(window_parts[:, 2], ((2, 0), (0, 0), (0, 0)))
    rims = jnp.concatenate([window_acc[0], window_acc[-1]], axis=0)
    returned = extended_2(rims, (("seq", 0),), BLOCK)
    totals = window_acc[1:-1]
    totals = totals.at[0].add(returned[:BLOCK]).at[-1].add(returned[-BLOCK:])
    for slot_idx, reach, inside, local_index in routes:
        back = shifted(extra[:, slot_idx], "seq", -reach)
        back = jnp.where(inside[:, None, None], back, 0.0)
        onehot = ((local_index[:, None] == block_range[None, :]) & inside[:, None]).astype(
            jnp.float32
        )
        totals = totals + jnp.einsum("jo,jbf->obf", onehot, back, precision=lax.Precision.HIGHEST)
    global_total = lax.psum(global_acc, "seq")
    owners = ((offsets[:, None] == block_range[None, :]) & (roots[:, None] == position)).astype(
        jnp.float32
    )
    totals = totals + jnp.einsum(
        "go,gbf->obf", owners, global_total, precision=lax.Precision.HIGHEST
    )
    flat = totals.reshape(rows, 2 * width)
    return (
        grad_query.reshape(rows, width),
        flat[:, :width].astype(jnp.bfloat16),
        flat[:, width:].astype(jnp.bfloat16),
    )


def solution(mesh):
    return jax.shard_map(
        on_device,
        mesh=mesh,
        in_specs=(
            P(("doc", "seq"), None),
            P(("doc", "seq"), None),
            P(("doc", "seq"), None),
            P(("doc", "seq"), None),
            P("doc", None),
            P("doc"),
        ),
        out_specs=(P(("doc", "seq"), None), P(("doc", "seq"), None), P(("doc", "seq"), None)),
        check_vma=False,
    )
```

profile of v0, /device:TPU:24, one launch (start us, length us, event | category | flops | bytes accessed | tf_op | source)
XLA Modules:
  0.0 2361.1 jit_solution(2911223016507517060)
XLA Ops:
  7.2 0.9 constant_dynamic-update-slice_fusion.4
  8.1 0.9 constant_dynamic-update-slice_fusion.3
  9.1 3.4 collective-permute-start
  12.5 4.6 collective-permute-start.1
  17.1 0.9 constant_dynamic-slice_fusion.7
  18.8 9.1 collective-permute-start.2
  28.6 7.9 collective-permute-start.3
  37.2 4.9 collective-permute-start.4
  49.0 0.7 select_bitcast_fusion
  52.0 0.6 compare_bitcast_fusion
  52.6 0.6 clamp_bitcast_fusion
  55.9 10.5 collective-permute-start.5
  66.5 1.9 collective-permute-start.6
  68.5 4.9 collective-permute-start.7
  73.5 48.9 %collective-permute-done.5 = bf16[2,64,1024]{2,1,0:T(8,128)(2,1)S(1)} collective-permute-done((bf16[2,64,1024]{2,1,0:T(8,128)(2,1)S(1)}, bf16[2,64,1024]{2,1,0:T(8,128)(2,1)S(1)}, u32[]{:S(2)}, u32[]{:S(2)}) %collective-permute-start.5) | collective-permute-done | bytes 262176 | tf_op jit(solution)/shard_map/ppermute | solution.py:30
  122.4 6.9 collective-permute-done.6
  129.3 11.5 collective-permute-done.7
  140.9 996.3 %all-reduce.9.cloned.1.call-done = (bf16[64,1024]{1,0:T(8,128)(2,1)}, bf16[64,1024]{1,0:T(8,128)(2,1)}) async-done(((bf16[64,1024]{1,0:T(8,128)(2,1)}, bf16[64,1024]{1,0:T(8,128)(2,1)}), (bf16[64,1024]{1,0:T(8,128)(2,1)}, bf16[64,1024]{1,0:T(8,128)(2,1)})) %all-reduce.9.cloned.1.call-update) | async-done | bytes 262160 | tf_op jit(solution)/shard_map/psum | solution.py:35
  1137.3 32.2 %while.22 = (s32[]{:T(128)}, f32[2,64,1024]{2,1,0:T(8,128)}, bf16[2,64,512]{2,1,0:T(8,128)(2,1)}, f32[2,3,64,1024]{3,2,0,1:T(8,128)}, f32[2,3,64,1024]{3,2,0,1:T...) while((s32[]{:T(128)}, f32[2,64,1024]{2,1,0:T(8,128)}, ...), condition=%wide.region_6.8_spmd.clone.clone, body=%wide.region_2.7_spmd.clone.clone.sunk | while | flops 209885696 | bytes 83506968 | solution.py:157
  1137.3 0.6 dynamic_slice.92
  1140.5 0.9 constant_dynamic-slice_fusion.12
  1141.5 0.9 constant_dynamic-slice_fusion.13
  1144.7 1.7 fusion.147
  1147.5 0.6 constant_dynamic-update-slice_fusion.7
  1148.9 0.9 copy-done
  1151.1 0.6 copy-done.1
  1151.7 1.1 copy-done.12
  1153.4 0.6 dynamic_slice.92
  1156.6 0.9 constant_dynamic-slice_fusion.12
  1157.6 0.9 constant_dynamic-slice_fusion.13
  1160.8 1.7 fusion.147
  1163.6 0.6 constant_dynamic-update-slice_fusion.7
  1165.0 0.9 copy-done
  1167.2 0.6 copy-done.1
  1167.8 1.1 copy-done.12
  1169.4 1.5 slice_bitcast_fusion.5
  1171.1 0.8 slice_bitcast_fusion.6
  1171.9 2.6 collective-permute-start.8
  1174.5 1.2 slice_bitcast_fusion.2
  1175.7 1.9 collective-permute-start.11
  1177.6 5.5 collective-permute-start.9
  1183.1 0.7 clamp_bitcast_fusion.5
  1183.8 1.9 collective-permute-start.10
  1185.7 1.2 copy.53
  1187.0 18.9 collective-permute-start.13
  1205.9 1.9 collective-permute-start.12
  1207.9 9.3 collective-permute-start.15
  1217.9 1.9 scatter-add.9
  1219.8 68.5 %collective-permute-done.11 = f32[2,64,1024]{2,1,0:T(8,128)S(1)} collective-permute-done((f32[2,64,1024]{2,1,0:T(8,128)}, f32[2,64,1024]{2,1,0:T(8,128)S(1)}, u32[]{:S(2)}, u32[]{:S(2)}) %collective-permute-start.11) | collective-permute-done | bytes 524320 | tf_op jit(solution)/shard_map/ppermute | solution.py:30
  1288.3 8.8 collective-permute-start.14
  1297.2 4.7 collective-permute-done.10
  1301.9 0.9 broadcast_select_fusion.4
  1302.9 1.2 broadcast_select_fusion.1
  1304.1 1.2 broadcast_select_fusion.2
  1305.3 1.3 fusion.41
  1306.8 1.3 fusion.37
  1308.1 1.3 fusion.39
  1309.4 6.8 collective-permute-done.14
  1316.4 1.3 fusion.33
  1317.7 1.3 fusion.35
  1319.0 1029.4 %all-reduce.7.cloned.1.call-done = f32[2,64,1024]{2,0,1:T(2,128)} async-done(((f32[2,64,1024]{2,0,1:T(2,128)}), f32[2,64,1024]{2,0,1:T(2,128)}) %all-reduce.7.cloned.1.call-update) | async-done | bytes 524304 | tf_op jit(solution)/shard_map/psum | solution.py:172
  2348.3 2.1 fusion.45
  2350.4 3.0 fusion.32
  2353.5 0.7 fusion.96
  (215 shorter events, 22.4 us)
Async XLA Ops:
  7.2 1130.1 %all-reduce.9.cloned.1.call-start = ((), (), s32[]{:S(2)}) async-start(), calls=%async_computation.1 | async-start | bytes 524288 | tf_op jit(solution)/shard_map/psum | solution.py:35
  9.1 46.9 %collective-permute-start = (bf16[64,1024]{1,0:T(8,128)(2,1)S(1)}, bf16[64,1024]{1,0:T(8,128)(2,1)S(1)}, u32[]{:S(2)}, u32[]{:S(2)}) collective-permute-start(bf16[64,1024]{1,0:T(8,128)(2,1)S(1)} %get-tuple-element.336), channel_id=1, source_target_pairs={{0,1},{1,2},{2,3},{3,4},{4,5},{5,6},{6,7},{7,8},{8,9},{9,10},{10,1... | collective-permute-start | bytes 393224 | tf_op jit(solution)/shard_map/ppermute | solution.py:19
  12.5 54.0 %collective-permute-start.1 = (bf16[64,1024]{1,0:T(8,128)(2,1)S(1)}, bf16[64,1024]{1,0:T(8,128)(2,1)S(1)}, u32[]{:S(2)}, u32[]{:S(2)}) collective-permute-start(bf16[64,1024]{1,0:T(8,128)(2,1)S(1)} %get-tuple-element.337), channel_id=1, source_target_pairs={{1,0},{2,1},{3,2},{4,3},{5,4},{6,5},{7,6},{8,7},{9,8},{10,9},{11,1... | collective-permute-start | bytes 393224 | tf_op jit(solution)/shard_map/ppermute | solution.py:22
  18.0 37.3 %copy-start.22 = (s32[2,3]{0,1:T(4,128)}, s32[2,3]{0,1:T(4,128)S(1)}, u32[]{:S(2)}) copy-start(s32[2,3]{0,1:T(4,128)S(1)} %get-tuple-element.341) | copy-start | bytes 76
  18.1 24.1 %copy-start.34 = (s32[2]{0:T(128)S(1)}, s32[2]{0:T(128)}, u32[]{:S(2)}) copy-start(s32[2]{0:T(128)} %param.19) | copy-start | bytes 28
  18.8 49.7 %collective-permute-start.2 = (bf16[2,64,1024]{2,1,0:T(8,128)(2,1)S(1)}, bf16[2,64,1024]{2,1,0:T(8,128)(2,1)S(1)}, u32[]{:S(2)}, u32[]{:S(2)}) collective-permute-start(bf16[2,64,1024]{2,1,0:T(8,128)(2,1)S(1)} %select_select_fusion.5), channel_id=1, source_target_pairs={{96,0},{97,1},{98,2},{99,3},{100,4},{101,5},{102,6},{103,7},{104,8... | collective-permute-start | bytes 786440 | tf_op jit(solution)/shard_map/ppermute | solution.py:30
  28.6 44.9 %collective-permute-start.3 = (bf16[2,64,1024]{2,1,0:T(8,128)(2,1)S(1)}, bf16[2,64,1024]{2,1,0:T(8,128)(2,1)S(1)}, u32[]{:S(2)}, u32[]{:S(2)}) collective-permute-start(bf16[2,64,1024]{2,1,0:T(8,128)(2,1)S(1)} %select_select_fusion.4), channel_id=1, source_target_pairs={{95,0},{96,1},{97,2},{98,3},{99,4},{100,5},{101,6},{102,7},{103,8}... | collective-permute-start | bytes 786440 | tf_op jit(solution)/shard_map/ppermute | solution.py:30
  36.5 18.7 copy-start.16
  37.2 36.3 %collective-permute-start.4 = (bf16[2,64,1024]{2,1,0:T(8,128)(2,1)S(1)}, bf16[2,64,1024]{2,1,0:T(8,128)(2,1)S(1)}, u32[]{:S(2)}, u32[]{:S(2)}) collective-permute-start(bf16[2,64,1024]{2,1,0:T(8,128)(2,1)S(1)} %select_select_fusion.3), channel_id=1, source_target_pairs={{64,0},{65,1},{66,2},{67,3},{68,4},{69,5},{70,6},{71,7},{72,8},{73... | collective-permute-start | bytes 786440 | tf_op jit(solution)/shard_map/ppermute | solution.py:30
  49.7 2298.6 %all-reduce.7.cloned.1.call-start = ((), (), s32[]{:S(2)}) async-start(), calls=%async_computation | async-start | bytes 1048576 | tf_op jit(solution)/shard_map/psum | solution.py:172
  53.2 2.2 copy-start.18
  53.2 2.2 copy-start.20
  55.9 66.4 %collective-permute-start.5 = (bf16[2,64,1024]{2,1,0:T(8,128)(2,1)S(1)}, bf16[2,64,1024]{2,1,0:T(8,128)(2,1)S(1)}, u32[]{:S(2)}, u32[]{:S(2)}) collective-permute-start(bf16[2,64,1024]{2,1,0:T(8,128)(2,1)S(1)} %select_select_fusion.2), channel_id=1, source_target_pairs={{63,0},{64,1},{65,2},{66,3},{67,4},{68,5},{69,6},{70,7},{71,8},{72... | collective-permute-start | bytes 786440 | tf_op jit(solution)/shard_map/ppermute | solution.py:30
  66.5 62.8 %collective-permute-start.6 = (bf16[2,64,1024]{2,1,0:T(8,128)(2,1)S(1)}, bf16[2,64,1024]{2,1,0:T(8,128)(2,1)S(1)}, u32[]{:S(2)}, u32[]{:S(2)}) collective-permute-start(bf16[2,64,1024]{2,1,0:T(8,128)(2,1)S(1)} %select_select_fusion.1), channel_id=1, source_target_pairs={{32,0},{33,1},{34,2},{35,3},{36,4},{37,5},{38,6},{39,7},{40,8},{41... | collective-permute-start | bytes 786440 | tf_op jit(solution)/shard_map/ppermute | solution.py:30
  68.5 72.3 %collective-permute-start.7 = (bf16[2,64,1024]{2,1,0:T(8,128)(2,1)S(1)}, bf16[2,64,1024]{2,1,0:T(8,128)(2,1)S(1)}, u32[]{:S(2)}, u32[]{:S(2)}) collective-permute-start(bf16[2,64,1024]{2,1,0:T(8,128)(2,1)S(1)} %select_select_fusion), channel_id=1, source_target_pairs={{31,0},{32,1},{33,2},{34,3},{35,4},{36,5},{37,6},{38,7},{39,8},{40... | collective-permute-start | bytes 786440 | tf_op jit(solution)/shard_map/ppermute | solution.py:30
  1137.3 3.2 copy-start.35
  1137.3 5.3 copy-start.5
  1137.3 5.4 copy-start.3
  1137.3 5.3 copy-start.9
  1137.3 5.3 copy-start.10
  1144.7 2.0 copy-start.39
  1148.9 1.9 copy-start.11
  1150.8 2.5 copy-start.4
  1150.9 2.5 copy-start.6
  1150.9 2.5 copy-start.36
  1151.7 1.7 copy-start.15
  1153.3 3.3 copy-start.35
  1153.3 5.3 copy-start.5
  1153.4 5.4 copy-start.3
  1153.4 5.3 copy-start.9
  1153.4 5.3 copy-start.10
  1160.8 2.0 copy-start.39
  1165.0 1.9 copy-start.11
  1167.0 2.5 copy-start.4
  1167.0 2.5 copy-start.6
  1167.0 2.5 copy-start.36
  1171.0 3.5 copy-start.13
  1171.1 14.6 copy-start.7
  1171.9 34.0 %collective-permute-start.8 = (f32[64,1024]{1,0:T(8,128)}, f32[64,1024]{1,0:T(8,128)S(1)}, u32[]{:S(2)}, u32[]{:S(2)}) collective-permute-start(f32[64,1024]{1,0:T(8,128)} %get-tuple-element.331), channel_id=1, source_target_pairs={{0,1},{1,2},{2,3},{3,4},{4,5},{5,6},{6,7},{7,8},{8,9},{9,10},{10,1... | collective-permute-start | bytes 786440 | tf_op jit(solution)/shard_map/ppermute | solution.py:19
  1174.5 11.2 copy-start.2
  1175.7 112.6 %collective-permute-start.11 = (f32[2,64,1024]{2,1,0:T(8,128)}, f32[2,64,1024]{2,1,0:T(8,128)S(1)}, u32[]{:S(2)}, u32[]{:S(2)}) collective-permute-start(f32[2,64,1024]{2,1,0:T(8,128)} %get-tuple-element.327), channel_id=1, source_target_pairs={{33,0},{34,1},{35,2},{36,3},{37,4},{38,5},{39,6},{40,7},{41,8},{42... | collective-permute-start | bytes 1572872 | tf_op jit(solution)/shard_map/ppermute | solution.py:30
  1177.6 30.3 %collective-permute-start.9 = (f32[64,1024]{1,0:T(8,128)S(1)}, f32[64,1024]{1,0:T(8,128)S(1)}, u32[]{:S(2)}, u32[]{:S(2)}) collective-permute-start(f32[64,1024]{1,0:T(8,128)S(1)} %get-tuple-element.330), channel_id=1, source_target_pairs={{1,0},{2,1},{3,2},{4,3},{5,4},{6,5},{7,6},{8,7},{9,8},{10,9},{11,1... | collective-permute-start | bytes 786440 | tf_op jit(solution)/shard_map/ppermute | solution.py:22
  1183.8 118.1 %collective-permute-start.10 = (f32[2,64,1024]{2,1,0:T(8,128)}, f32[2,64,1024]{2,1,0:T(8,128)S(1)}, u32[]{:S(2)}, u32[]{:S(2)}) collective-permute-start(f32[2,64,1024]{2,1,0:T(8,128)} %get-tuple-element.327), channel_id=1, source_target_pairs={{32,0},{33,1},{34,2},{35,3},{36,4},{37,5},{38,6},{39,7},{40,8},{41... | collective-permute-start | bytes 1572872 | tf_op jit(solution)/shard_map/ppermute | solution.py:30
  1185.7 22.1 copy-start.8
  1185.7 22.1 slice-start
  1187.0 115.9 %collective-permute-start.13 = (f32[2,64,1024]{2,1,0:T(8,128)}, f32[2,64,1024]{2,1,0:T(8,128)}, u32[]{:S(2)}, u32[]{:S(2)}) collective-permute-start(f32[2,64,1024]{2,1,0:T(8,128)} %get-tuple-element.328), channel_id=1, source_target_pairs={{65,0},{66,1},{67,2},{68,3},{69,4},{70,5},{71,6},{72,7},{73,8},{74... | collective-permute-start | bytes 1572872 | tf_op jit(solution)/shard_map/ppermute | solution.py:30
  1205.9 98.2 %collective-permute-start.12 = (f32[2,64,1024]{2,1,0:T(8,128)}, f32[2,64,1024]{2,1,0:T(8,128)}, u32[]{:S(2)}, u32[]{:S(2)}) collective-permute-start(f32[2,64,1024]{2,1,0:T(8,128)} %get-tuple-element.328), channel_id=1, source_target_pairs={{64,0},{65,1},{66,2},{67,3},{68,4},{69,5},{70,6},{71,7},{72,8},{73... | collective-permute-start | bytes 1572872 | tf_op jit(solution)/shard_map/ppermute | solution.py:30
  1207.9 98.7 %collective-permute-start.15 = (f32[2,64,1024]{2,1,0:T(8,128)}, f32[2,64,1024]{2,1,0:T(8,128)S(1)}, u32[]{:S(2)}, u32[]{:S(2)}) collective-permute-start(f32[2,64,1024]{2,1,0:T(8,128)} %get-tuple-element.329), channel_id=1, source_target_pairs={{97,0},{98,1},{99,2},{100,3},{101,4},{102,5},{103,6},{104,7},{105,... | collective-permute-start | bytes 1572872 | tf_op jit(solution)/shard_map/ppermute | solution.py:30
  1217.9 84.9 %copy-start.17 = (pred[2]{0:T(512)(128)(4,1)S(1)}, pred[2]{0:T(512)(128)(4,1)}, u32[]{:S(2)}) copy-start(pred[2]{0:T(512)(128)(4,1)} %copy-done.16) | copy-start | bytes 10
  1288.3 27.9 %collective-permute-start.14 = (f32[2,64,1024]{2,1,0:T(8,128)}, f32[2,64,1024]{2,1,0:T(8,128)S(1)}, u32[]{:S(2)}, u32[]{:S(2)}) collective-permute-start(f32[2,64,1024]{2,1,0:T(8,128)} %get-tuple-element.329), channel_id=1, source_target_pairs={{96,0},{97,1},{98,2},{99,3},{100,4},{101,5},{102,6},{103,7},{104,8... | collective-permute-start | bytes 1572872 | tf_op jit(solution)/shard_map/ppermute | solution.py:30
  1297.2 8.0 copy-start.32
  1297.2 8.0 copy-start.33
  1302.9 3.7 copy-start.21
  1304.0 2.7 copy-start.30
  1304.0 2.7 copy-start.31
  1305.2 2.8 copy-start.28
  1305.3 2.8 copy-start.29
  1306.6 9.6 copy-start.19
  1306.7 9.6 copy-start.26
  1306.8 9.6 copy-start.27
  1308.1 9.6 copy-start.24
  1308.1 9.6 copy-start.25
  1309.4 1038.9 %copy-start.23 = (pred[2]{0:T(512)(128)(4,1)S(1)}, pred[2]{0:T(512)(128)(4,1)}, u32[]{:S(2)}) copy-start(pred[2]{0:T(512)(128)(4,1)} %get-tuple-element.302) | copy-start | bytes 10
  1316.3 1034.1 %copy-start.37 = (pred[2]{0:T(512)(128)(4,1)S(1)}, pred[2]{0:T(512)(128)(4,1)}, u32[]{:S(2)}) copy-start(pred[2]{0:T(512)(128)(4,1)} %compare_bitcast_fusion.5) | copy-start | bytes 10
  (11 other events, 12.8 us)
Sparse Core Ops, SparseCore 0:
  49.8 1087.3 all-reduce.8
  1187.1 1161.2 all-reduce.6
where the time goes:
time: 2370 us; the launch traced here: 2360 us
  waiting for transfers between devices  2170 us (92%)
  starting transfers between devices  98.1 us (4%)
  local copies, waits for them, and re-layouts  33.9 us (1%)
    psum x1, waiting for transfers between devices, on_device(): global_total = lax.psum(global_acc, 'seq')  1030 us
    psum x1, waiting for transfers between devices, broadcast(): return lax.psum(block, axis)  996 us
    ppermute x12, waiting for transfers between devices, shifted(): return lax.ppermute(block, axis, route)  147 us
    ppermute x12, starting transfers between devices, shifted(): return lax.ppermute(block, axis, route)  82 us
  transfers between devices with their start and end apart: 18, of which 8 were waited for; matrix products, arithmetic and copies ran while one was open for 1% of the time, Pallas kernels for 0%

commit v1 on v0

v1 whole, which is shorter than its diff:
```python
import functools

import jax
import jax.numpy as jnp
from jax import lax
from jax.experimental import pallas as pl
from jax.experimental.pallas import tpu as pltpu
from jax.sharding import PartitionSpec as P

MESH = pl.DeviceIdType.MESH
BLOCK = 64
RAND = 3
GLOBAL = 2
PARTS = 4
PLANE = 8
LAYERS = 4
GROUPS = PLANE * LAYERS
SEQ = PARTS * GROUPS
W = 128
HALF = 64
BF = jnp.bfloat16
F32 = jnp.float32


def kernel(
    q_hbm, k_hbm, v_hbm, do_hbm, pick_ref, gid_ref,
    dq_out, dk_out, dv_out,
    q_all, do_all, kv_own, kv_left, kv_right,
    cand, g1, g2, kv_glob,
    acc_own, acc_left, acc_right, acc_glob,
    edge_out, edge_in, h1, h2, tot_glob,
    dq_stage, dk_stage, dv_stage,
    in_send, in_recv, edge_send, edge_recv, g_send, g_recv,
    dq_send, dq_recv, dkv_send, dkv_recv,
):
    me = lax.axis_index("seq")
    part = lax.div(me, GROUPS)
    group = lax.rem(me, GROUPS)
    layer = lax.div(group, PLANE)
    spot = lax.rem(group, PLANE)

    def mate(quarter):
        return {"seq": quarter * GROUPS + group}

    def in_plane(other):
        return {"seq": part * GROUPS + layer * PLANE + other}

    def in_layer(other):
        return {"seq": part * GROUPS + other * PLANE + spot}

    right = {"seq": part * GROUPS + lax.rem(group + 1, GROUPS)}
    left = {"seq": part * GROUPS + lax.rem(group + GROUPS - 1, GROUPS)}

    barrier = pltpu.get_barrier_semaphore()

    def greet(where):
        pl.semaphore_signal(barrier, inc=1, device_id=where, device_id_type=MESH)

    for j in range(1, PARTS):
        greet(mate(lax.rem(part + j, PARTS)))
    greet(left)
    greet(right)
    for o in range(1, PLANE):
        greet(in_plane(lax.rem(spot + o, PLANE)))
    for o in range(1, LAYERS):
        greet(in_layer(lax.rem(layer + o, LAYERS)))
    pl.semaphore_wait(barrier, PARTS - 1 + 2 + PLANE - 1 + LAYERS - 1)

    def remote(src, dst, send, recv, where):
        return pltpu.make_async_remote_copy(
            src_ref=src, dst_ref=dst, send_sem=send, recv_sem=recv, device_id=where,
            device_id_type=MESH,
        )

    two = 2 * W

    def cols(quarter):
        return pl.ds(pl.multiple_of(quarter * W, W), W)

    arrays = (
        (k_hbm, lambda s: kv_own.at[s, :, 0:W]),
        (v_hbm, lambda s: kv_own.at[s, :, W : 2 * W]),
        (q_hbm, lambda s: q_all.at[s]),
        (do_hbm, lambda s: do_all.at[s]),
    )

    def incoming(n, j):
        hbm, place = arrays[n]
        to = lax.rem(part + j, PARTS)
        return remote(
            hbm.at[:, cols(to)], place(part), in_send.at[n, j], in_recv.at[n, j], mate(to)
        )

    def own_copy(n):
        hbm, place = arrays[n]
        return pltpu.make_async_copy(hbm.at[:, cols(part)], place(part), in_recv.at[n, 0])

    for n in range(4):
        for j in (2, 1, 3):
            incoming(n, j).start()
        own_copy(n).start()

    acc_own[...] = jnp.zeros_like(acc_own)
    acc_left[...] = jnp.zeros_like(acc_left)
    acc_right[...] = jnp.zeros_like(acc_right)
    acc_glob[...] = jnp.zeros_like(acc_glob)

    for n in range(2):
        own_copy(n).wait()
        for j in (1, 3, 2):
            incoming(n, j).wait_recv()

    to_right = remote(
        kv_own.at[:, BLOCK : 2 * BLOCK, :], kv_left, edge_send.at[0], edge_recv.at[0], right
    )
    to_left = remote(
        kv_own.at[:, 0:BLOCK, :], kv_right, edge_send.at[1], edge_recv.at[1], left
    )
    to_right.start()
    to_left.start()

    def choose(code, options):
        code = jnp.full((1, two), code, jnp.int32)
        total = None
        for n, option in enumerate(options):
            option = option.astype(F32)
            term = jnp.where(code == n, option, jnp.zeros_like(option))
            total = term if total is None else total + term
        return total.astype(BF)

    for m in range(GLOBAL):
        gid = gid_ref[m]
        cand[m * BLOCK : (m + 1) * BLOCK, :] = choose(
            lax.div(gid, 2 * GROUPS) * 2 + lax.rem(gid, 2),
            [kv_own[s, b * BLOCK : (b + 1) * BLOCK, :] for s in range(PARTS) for b in range(2)],
        )

    def rows(t):
        return pl.ds(pl.multiple_of(t * 16, 16), 16)

    my_gid = gid_ref[lax.div(spot, PLANE // GLOBAL)]
    gid_spot = lax.rem(lax.div(my_gid, 2), PLANE)
    gid_layer = lax.rem(lax.div(my_gid, 2 * PLANE), LAYERS)

    def scatter_plane(source, slots, base):
        def copy(o):
            to = lax.rem(spot + o, PLANE)
            return remote(
                source.at[rows(to)], slots.at[spot], g_send.at[base, o], g_recv.at[base, o],
                in_plane(to),
            )
        return copy

    def spread_layers(slots, base):
        def copy(o):
            to = lax.rem(layer + o, LAYERS)
            return remote(
                slots.at[layer], slots.at[layer], g_send.at[base, o], g_recv.at[base, o],
                in_layer(to),
            )
        return copy

    def gather_plane(whole, base):
        def copy(o):
            to = lax.rem(spot + o, PLANE)
            return remote(
                whole.at[rows(spot)], whole.at[rows(spot)], g_send.at[base, o],
                g_recv.at[base, o], in_plane(to),
            )
        return copy

    def start_all(copy, count):
        def step(o, _):
            copy(o).start()
            return 0
        lax.fori_loop(1, count, step, 0)

    def wait_all(copy, count):
        def step(o, _):
            copy(o).wait()
            return 0
        lax.fori_loop(1, count, step, 0)

    c1 = scatter_plane(cand, g1, 0)
    start_all(c1, PLANE)
    g1[spot] = cand[rows(spot), :]
    wait_all(c1, PLANE)
    g2[layer] = choose(gid_spot, [g1[t] for t in range(PLANE)])
    c2 = spread_layers(g2, 1)
    start_all(c2, LAYERS)
    wait_all(c2, LAYERS)
    kv_glob[rows(spot), :] = choose(gid_layer, [g2[t] for t in range(LAYERS)])
    c3 = gather_plane(kv_glob, 2)
    start_all(c3, PLANE)
    wait_all(c3, PLANE)

    to_right.wait()
    to_left.wait()

    first_group = (group == 0).astype(jnp.int32)
    last_group = (group == GROUPS - 1).astype(jnp.int32)
    low = lax.broadcasted_iota(jnp.int32, (BLOCK, W), 1) < HALF

    def two_heads(x):
        x = x.astype(F32)
        zero = jnp.zeros_like(x)
        return jnp.concatenate([jnp.where(low, x, zero), jnp.where(low, zero, x)], axis=0)

    def dot(a, b, dims):
        return lax.dot_general(a, b, (dims, ((), ())), preferred_element_type=F32)

    def outgoing_dq(j):
        to = lax.rem(part + j, PARTS)
        return remote(
            dq_stage.at[to], dq_out.at[:, cols(part)], dq_send.at[j], dq_recv.at[j], mate(to)
        )

    def own_dq():
        return pltpu.make_async_copy(dq_stage.at[part], dq_out.at[:, cols(part)], dq_recv.at[0])

    def visit(t, _):
        j = t + t // 2 - 2 * (t // 3)
        here = lax.rem(part + PARTS - j, PARTS)
        for n in (2, 3):
            @pl.when(j == 0)
            def _():
                own_copy(n).wait()

            @pl.when(j != 0)
            def _():
                incoming(n, j).wait_recv()

        at_left = lax.rem(here + (PARTS - 1) * first_group, PARTS)
        at_right = lax.rem(here + last_group, PARTS)
        for b in range(2):
            number = here * (2 * GROUPS) + 2 * group + b
            own0 = (kv_own, here, 0, acc_own)
            own1 = (kv_own, here, BLOCK, acc_own)
            window = [
                (kv_left, at_left, 0, acc_left) if b == 0 else own0,
                own0 if b == 0 else own1,
                own1 if b == 0 else (kv_right, at_right, 0, acc_right),
            ]
            def load(entry):
                ref, s, start, _ = entry
                return ref[s, start : start + BLOCK, :]

            def add(entry, value):
                _, s, start, acc = entry
                acc[s, start : start + BLOCK, :] += value

            choices = []
            taken = []
            pieces = [load(e) for e in window]
            pieces.append(kv_glob[...])
            for s in range(RAND):
                far = lax.rem(here + PARTS - (s + 1), PARTS)
                far_left = lax.rem(far + (PARTS - 1) * first_group, PARTS)
                pick = jnp.full((1, two), pick_ref[s, number].astype(F32)).astype(BF)
                near_entry = (kv_own, far, b * BLOCK, acc_own)
                far_entry = (kv_left, far_left, 0, acc_left) if b == 0 else (kv_own, far, 0, acc_own)
                choices.append((near_entry, far_entry))
                taken.append(pick)
                pieces.append(load(near_entry) * (1 - pick) + load(far_entry) * pick)
            listed = jnp.concatenate(pieces, axis=0)
            keys = listed[:, 0:W]
            values = listed[:, W : 2 * W]
            q2 = (two_heads(q_all[here, b * BLOCK : (b + 1) * BLOCK, :]) * 0.125).astype(BF)
            do2 = two_heads(do_all[here, b * BLOCK : (b + 1) * BLOCK, :]).astype(BF)
            scores = dot(keys, q2, ((1,), (1,)))
            if b == 0:
                masked = jnp.where(number == 0, -1e30, scores[:BLOCK])
                scores = jnp.concatenate([masked, scores[BLOCK:]], axis=0)
            else:
                masked = jnp.where(number == 2 * SEQ - 1, -1e30, scores[2 * BLOCK : 3 * BLOCK])
                scores = jnp.concatenate(
                    [scores[: 2 * BLOCK], masked, scores[3 * BLOCK :]], axis=0
                )
            row_max = jnp.max(scores, axis=0, keepdims=True)
            expo = jnp.exp(scores - row_max)
            row_total = jnp.sum(expo, axis=0, keepdims=True)
            probs = expo * (1.0 / row_total)
            probs_half = probs.astype(BF)
            grad_probs = dot(values, do2, ((1,), (1,)))
            row_dot = jnp.sum(probs_half.astype(F32) * grad_probs, axis=0, keepdims=True)
            grad_half = (probs * (grad_probs - row_dot)).astype(BF)
            back = dot(grad_half, keys, ((0,), (0,)))
            dq_stage[here, b * BLOCK : (b + 1) * BLOCK, :] = (
                jnp.where(low, back[:BLOCK], back[BLOCK:]) * 0.125
            ).astype(BF)
            grads = jnp.concatenate(
                [dot(grad_half, q2, ((1,), (0,))), dot(probs_half, do2, ((1,), (0,)))], axis=1
            )
            for n, entry in enumerate(window):
                add(entry, grads[n * BLOCK : (n + 1) * BLOCK])
            acc_glob[...] += grads[3 * BLOCK : (3 + GLOBAL) * BLOCK]
            for s in range(RAND):
                part_grad = grads[(3 + GLOBAL + s) * BLOCK : (4 + GLOBAL + s) * BLOCK]
                near_entry, far_entry = choices[s]
                far_grad = part_grad * taken[s].astype(F32)
                add(near_entry, part_grad - far_grad)
                add(far_entry, far_grad)

        @pl.when(j == 0)
        def _():
            own_dq().start()

        @pl.when(j != 0)
        def _():
            outgoing_dq(PARTS - j).start()

        return 0

    lax.fori_loop(0, PARTS, visit, 0)

    c4 = scatter_plane(acc_glob, h1, 3)
    start_all(c4, PLANE)
    edge_out[0] = acc_left[...].astype(BF)
    edge_out[1] = acc_right[...].astype(BF)
    back_left = remote(edge_out.at[0], edge_in.at[0], edge_send.at[2], edge_recv.at[2], left)
    back_right = remote(edge_out.at[1], edge_in.at[1], edge_send.at[3], edge_recv.at[3], right)
    back_left.start()
    back_right.start()
    h1[spot] = acc_glob[rows(spot), :]
    wait_all(c4, PLANE)
    h2[layer] = jnp.sum(h1[...], axis=0)
    c5 = spread_layers(h2, 4)
    start_all(c5, LAYERS)
    wait_all(c5, LAYERS)
    tot_glob[rows(spot), :] = jnp.sum(h2[...], axis=0)
    c6 = gather_plane(tot_glob, 5)
    start_all(c6, PLANE)

    back_left.wait()
    back_right.wait()
    acc_own[:, BLOCK : 2 * BLOCK, :] += edge_in[0].astype(F32)
    acc_own[:, 0:BLOCK, :] += edge_in[1].astype(F32)
    wait_all(c6, PLANE)

    def outgoing(stage, out, n, j):
        to = lax.rem(part + j, PARTS)
        return remote(
            stage.at[to], out.at[:, cols(part)], dkv_send.at[n, j], dkv_recv.at[n, j], mate(to)
        )

    def own_out(stage, out, n):
        return pltpu.make_async_copy(stage.at[part], out.at[:, cols(part)], dkv_recv.at[n, 0])

    results = ((dk_stage, dk_out), (dv_stage, dv_out))
    for j in (2, 1, 3, 0):
        there = lax.rem(part + j, PARTS)
        for b in range(2):
            number = there * (2 * GROUPS) + 2 * group + b
            total = acc_own[there, b * BLOCK : (b + 1) * BLOCK, :]
            for m in range(GLOBAL):
                extra = tot_glob[m * BLOCK : (m + 1) * BLOCK, :]
                named = jnp.full((1, two), gid_ref[m], jnp.int32) == number
                total = total + jnp.where(named, extra, jnp.zeros_like(extra))
            dk_stage[there, b * BLOCK : (b + 1) * BLOCK, :] = total[:, 0:W].astype(BF)
            dv_stage[there, b * BLOCK : (b + 1) * BLOCK, :] = total[:, W : 2 * W].astype(BF)
        for n, (stage, out) in enumerate(results):
            if j == 0:
                own_out(stage, out, n).start()
            else:
                outgoing(stage, out, n, j).start()

    for n in range(4):
        for j in range(1, PARTS):
            incoming(n, j).wait_send()
    own_dq().wait()
    for j in range(1, PARTS):
        outgoing_dq(j).wait()
    for n, (stage, out) in enumerate(results):
        own_out(stage, out, n).wait()
        for j in range(1, PARTS):
            outgoing(stage, out, n, j).wait()


def on_device(queries, key_vectors, value_vectors, output_grad, rand_pick, global_ids):
    rows, width = queries.shape
    out = jax.ShapeDtypeStruct((rows, width), BF)
    anywhere = pl.BlockSpec(memory_space=pl.ANY)
    small = pl.BlockSpec(memory_space=pltpu.SMEM)
    two = 2 * W
    scratch = [
        pltpu.VMEM((PARTS, 2 * BLOCK, W), BF),
        pltpu.VMEM((PARTS, 2 * BLOCK, W), BF),
        pltpu.VMEM((PARTS, 2 * BLOCK, two), BF),
        pltpu.VMEM((PARTS, BLOCK, two), BF),
        pltpu.VMEM((PARTS, BLOCK, two), BF),
        pltpu.VMEM((GLOBAL * BLOCK, two), BF),
        pltpu.VMEM((PLANE, 16, two), BF),
        pltpu.VMEM((LAYERS, 16, two), BF),
        pltpu.VMEM((GLOBAL * BLOCK, two), BF),
        pltpu.VMEM((PARTS, 2 * BLOCK, two), F32),
        pltpu.VMEM((PARTS, BLOCK, two), F32),
        pltpu.VMEM((PARTS, BLOCK, two), F32),
        pltpu.VMEM((GLOBAL * BLOCK, two), F32),
        pltpu.VMEM((2, PARTS, BLOCK, two), BF),
        pltpu.VMEM((2, PARTS, BLOCK, two), BF),
        pltpu.VMEM((PLANE, 16, two), F32),
        pltpu.VMEM((LAYERS, 16, two), F32),
        pltpu.VMEM((GLOBAL * BLOCK, two), F32),
        pltpu.VMEM((PARTS, 2 * BLOCK, W), BF),
        pltpu.VMEM((PARTS, 2 * BLOCK, W), BF),
        pltpu.VMEM((PARTS, 2 * BLOCK, W), BF),
        pltpu.SemaphoreType.DMA((4, PARTS)),
        pltpu.SemaphoreType.DMA((4, PARTS)),
        pltpu.SemaphoreType.DMA((4,)),
        pltpu.SemaphoreType.DMA((4,)),
        pltpu.SemaphoreType.DMA((6, PLANE)),
        pltpu.SemaphoreType.DMA((6, PLANE)),
        pltpu.SemaphoreType.DMA((PARTS,)),
        pltpu.SemaphoreType.DMA((PARTS,)),
        pltpu.SemaphoreType.DMA((2, PARTS)),
        pltpu.SemaphoreType.DMA((2, PARTS)),
    ]
    return pl.pallas_call(
        kernel,
        out_shape=(out, out, out),
        in_specs=[anywhere] * 4 + [small] * 2,
        out_specs=(anywhere,) * 3,
        scratch_shapes=scratch,
        compiler_params=pltpu.CompilerParams(
            collective_id=1, has_side_effects=True, vmem_limit_bytes=32 * 1024 * 1024
        ),
        name="sparse_attention_grads",
    )(queries, key_vectors, value_vectors, output_grad, rand_pick.T, global_ids)


def solution(mesh):
    spec = P(("doc", "seq"), None)
    return jax.shard_map(
        on_device,
        mesh=mesh,
        in_specs=(spec, spec, spec, spec, P("doc", None), P("doc")),
        out_specs=(spec, spec, spec),
        check_vma=False,
    )
```

time: 2370 us -> 88.8 us (0.04)
  waiting for transfers between devices: 2170 us -> 0 us
  starting transfers between devices: 98.1 us -> 0 us
  Pallas kernels: 0 us -> 80.4 us
  local copies, waits for them, and re-layouts: 33.9 us -> 6.92 us
    psum x2 -> x0, waiting for transfers between devices: 2030 us -> none  [the longest x1 1030 us: on_device(): global_total = lax.psum(global_acc, 'seq')]
    ppermute x16 -> x0, waiting for transfers between devices: 147 us -> none  [the longest x12 147 us: shifted(): return lax.ppermute(block, axis, route)]
    ppermute x16 -> x0, starting transfers between devices: 98 us -> none  [the longest x12 82 us: shifted(): return lax.ppermute(block, axis, route)]
    pallas_call x0 -> x1, Pallas kernels: none -> 80.4 us  [on_device(): pl.pallas_call(kernel, out_shape=(out, out, out), in_specs=[anywhere] * 4...]
  transfers between devices with their start and end apart: 18 -> 0, of which waited for: 8 -> 0; matrix products, arithmetic and copies ran while one was open for 1% -> 0% of each run, Pallas kernels for 0% -> 0%
where the time goes in v1:
time: 88.8 us; the launch traced here: 87.9 us
  Pallas kernels  80.4 us (91%)
  local copies, waits for them, and re-layouts  6.92 us (8%)
    pallas_call x1, Pallas kernels, on_device(): pl.pallas_call(kernel, out_shape=(out, out, out), in_specs=[anywhere] * 4...  80.4 us
    unnamed x15, local copies, waits for them, and re-layouts  6.92 us

profile of v1, /device:TPU:24, one launch (start us, length us, event | category | flops | bytes accessed | tf_op | source)
XLA Modules:
  0.0 87.9 jit_solution(3358412670465311205)
XLA Ops:
  0.6 0.0 copy-start.5
  0.6 0.6 copy-done.5
  1.3 0.0 copy-start
  1.3 0.9 %copy-done = bf16[128,512]{1,0:T(8,128)(2,1)S(1)} copy-done((bf16[128,512]{1,0:T(8,128)(2,1)S(1)}, bf16[128,512]{1,0:T(8,128)(2,1)}, u32[]{:S(2)}) %copy-start) | copy-done | bytes 131096
  2.2 0.0 copy-start.1
  2.2 0.9 %copy-done.1 = bf16[128,512]{1,0:T(8,128)(2,1)S(1)} copy-done((bf16[128,512]{1,0:T(8,128)(2,1)S(1)}, bf16[128,512]{1,0:T(8,128)(2,1)}, u32[]{:S(2)}) %copy-start.1) | copy-done | bytes 131096
  3.1 0.0 copy-start.2
  3.1 0.9 %copy-done.2 = bf16[128,512]{1,0:T(8,128)(2,1)S(1)} copy-done((bf16[128,512]{1,0:T(8,128)(2,1)S(1)}, bf16[128,512]{1,0:T(8,128)(2,1)}, u32[]{:S(2)}) %copy-start.2) | copy-done | bytes 131096
  4.0 0.0 copy-start.3
  4.0 0.9 %copy-done.3 = bf16[128,512]{1,0:T(8,128)(2,1)S(1)} copy-done((bf16[128,512]{1,0:T(8,128)(2,1)S(1)}, bf16[128,512]{1,0:T(8,128)(2,1)}, u32[]{:S(2)}) %copy-start.3) | copy-done | bytes 131096
  4.9 0.0 copy-start.4
  4.9 0.7 copy-done.4
  5.6 80.4 %sparse_attention_grads.1 = (bf16[128,512]{1,0:T(8,128)(2,1)S(1)}, bf16[128,512]{1,0:T(8,128)(2,1)S(1)}, bf16[128,512]{1,0:T(8,128)(2,1)S(1)}) custom-call(bf16[128,512]{1,0:T(8,128)(2,1)S(1)} %copy-done, bf16[128,512]{1,0:T(8,128)(2,1)S(1)} %copy-done.1, bf16[128,512]{1,0:T(8,128)(2,1)S(1)} %copy-done.2, bf16[128,512]{1,0:T(8,128)(2,1)S(1)} %copy-done.3, ...), custom_call_target="tpu_custom_call" | custom-call | tf_op jit(solution)/shard_map/sparse_attention_grads/pallas_call | solution.py:418
  86.0 0.7 copy.12
  86.6 0.7 copy.13
  87.3 0.7 copy.14
Async XLA Ops:
  0.6 0.7 copy-start.5
  1.3 0.9 %copy-start = (bf16[128,512]{1,0:T(8,128)(2,1)S(1)}, bf16[128,512]{1,0:T(8,128)(2,1)}, u32[]{:S(2)}) copy-start(bf16[128,512]{1,0:T(8,128)(2,1)} %q_hbm.1) | copy-start | bytes 393220
  2.2 0.9 %copy-start.1 = (bf16[128,512]{1,0:T(8,128)(2,1)S(1)}, bf16[128,512]{1,0:T(8,128)(2,1)}, u32[]{:S(2)}) copy-start(bf16[128,512]{1,0:T(8,128)(2,1)} %k_hbm.1) | copy-start | bytes 393220
  3.1 0.9 %copy-start.2 = (bf16[128,512]{1,0:T(8,128)(2,1)S(1)}, bf16[128,512]{1,0:T(8,128)(2,1)}, u32[]{:S(2)}) copy-start(bf16[128,512]{1,0:T(8,128)(2,1)} %v_hbm.1) | copy-start | bytes 393220
  4.0 0.9 %copy-start.3 = (bf16[128,512]{1,0:T(8,128)(2,1)S(1)}, bf16[128,512]{1,0:T(8,128)(2,1)}, u32[]{:S(2)}) copy-start(bf16[128,512]{1,0:T(8,128)(2,1)} %do_hbm.1) | copy-start | bytes 393220
  4.9 0.7 copy-start.4

commit v2 on v1

--- a/solution.py
+++ b/solution.py
@@ -18,6 +18,7 @@
 SEQ = PARTS * GROUPS
 W = 128
 HALF = 64
+FULL = PARTS * W
 BF = jnp.bfloat16
 F32 = jnp.float32
 
@@ -26,11 +27,11 @@
     q_hbm, k_hbm, v_hbm, do_hbm, pick_ref, gid_ref,
     dq_out, dk_out, dv_out,
     q_all, do_all, kv_own, kv_left, kv_right,
-    cand, g1, g2, kv_glob,
+    kv_raw, cand, g1, g2_out, g2, g3, kv_glob,
     acc_own, acc_left, acc_right, acc_glob,
-    edge_out, edge_in, h1, h2, tot_glob,
+    edge_out, edge_in, h1_out, h1, h2, h3,
     dq_stage, dk_stage, dv_stage,
-    in_send, in_recv, edge_send, edge_recv, g_send, g_recv,
+    raw_sem, in_send, in_recv, edge_send, edge_recv, g_send, g_recv,
     dq_send, dq_recv, dkv_send, dkv_recv,
 ):
     me = lax.axis_index("seq")
@@ -64,8 +65,6 @@
         greet(in_plane(lax.rem(spot + o, PLANE)))
     for o in range(1, LAYERS):
         greet(in_layer(lax.rem(layer + o, LAYERS)))
-    pl.semaphore_wait(barrier, PARTS - 1 + 2 + PLANE - 1 + LAYERS - 1)
-
     def remote(src, dst, send, recv, where):
         return pltpu.make_async_remote_copy(
             src_ref=src, dst_ref=dst, send_sem=send, recv_sem=recv, device_id=where,
@@ -95,9 +94,12 @@
         hbm, place = arrays[n]
         return pltpu.make_async_copy(hbm.at[:, cols(part)], place(part), in_recv.at[n, 0])
 
+    def raw_copy(n):
+        return pltpu.make_async_copy((k_hbm, v_hbm)[n], kv_raw.at[n], raw_sem.at[n])
+
+    for n in range(2):
+        raw_copy(n).start()
     for n in range(4):
-        for j in (2, 1, 3):
-            incoming(n, j).start()
         own_copy(n).start()
 
     acc_own[...] = jnp.zeros_like(acc_own)
@@ -105,10 +107,58 @@
     acc_right[...] = jnp.zeros_like(acc_right)
     acc_glob[...] = jnp.zeros_like(acc_glob)
 
+    def choose(code, options):
+        code = jnp.full((1, options[0].shape[-1]), code, jnp.int32)
+        total = None
+        for n, option in enumerate(options):
+            option = option.astype(F32)
+            term = jnp.where(code == n, option, jnp.zeros_like(option))
+            total = term if total is None else total + term
+        return total.astype(BF)
+
+    def rows(t):
+        return pl.ds(pl.multiple_of(t * 16, 16), 16)
+
     for n in range(2):
-        own_copy(n).wait()
-        for j in (1, 3, 2):
-            incoming(n, j).wait_recv()
+        raw_copy(n).wait()
+    for t in range(PLANE):
+        odd = lax.rem(gid_ref[t // (PLANE // GLOBAL)], 2)
+        start = (t % (PLANE // GLOBAL)) * 16
+        for n in range(2):
+            cand[t, :, n * FULL : (n + 1) * FULL] = choose(
+                odd, [kv_raw[n, b * BLOCK + start : b * BLOCK + start + 16, :] for b in range(2)]
+            )
+
+    my_gid = gid_ref[lax.div(spot, PLANE // GLOBAL)]
+    gid_spot = lax.rem(lax.div(my_gid, 2), PLANE)
+    gid_layer = lax.rem(lax.div(my_gid, 2 * PLANE), LAYERS)
+    gid_part = lax.div(my_gid, 2 * GROUPS)
+
+    def around(base, count, here, where, source, place):
+        def copy(o):
+            to = lax.rem(here + o, count)
+            return remote(
+                source(to), place(here), g_send.at[base, o], g_recv.at[base, o], where(to)
+            )
+        return copy
+
+    finish = []
+
+    def start_all(copy, count):
+        for o in range(1, count):
+            copy(o).start()
+
+    def wait_all(copy, count):
+        for o in range(1, count):
+            copy(o).wait_recv()
+        finish.append((copy, count))
+
+    c1 = around(0, PLANE, spot, in_plane, lambda to: cand.at[to], lambda i: g1.at[i])
+    c2 = around(1, PARTS, part, mate, lambda to: g2_out.at[to], lambda i: g2.at[i])
+    c3 = around(2, LAYERS, layer, in_layer, lambda to: g3.at[layer], lambda i: g3.at[i])
+    c4 = around(
+        3, PLANE, spot, in_plane, lambda to: kv_glob.at[rows(spot)], lambda i: kv_glob.at[rows(i)]
+    )
 
     to_right = remote(
         kv_own.at[:, BLOCK : 2 * BLOCK, :], kv_left, edge_send.at[0], edge_recv.at[0], right
@@ -116,84 +166,46 @@
     to_left = remote(
         kv_own.at[:, 0:BLOCK, :], kv_right, edge_send.at[1], edge_recv.at[1], left
     )
+
+    pl.semaphore_wait(barrier, PARTS - 1 + 2 + PLANE - 1 + LAYERS - 1)
+
+
+    def send(n, j):
+        incoming(n, j).start()
+
+    start_all(c1, PLANE)
+    for j in (2, 1, 3):
+        send(0, j)
+    g1[spot] = cand[spot]
+    wait_all(c1, PLANE)
+    piece = choose(gid_spot, [g1[t] for t in range(PLANE)])
+    for h in range(PARTS):
+        g2_out[h, :, 0:W] = piece[:, h * W : (h + 1) * W]
+        g2_out[h, :, W:two] = piece[:, FULL + h * W : FULL + (h + 1) * W]
+    start_all(c2, PARTS)
+    for j in (2, 1, 3):
+        send(1, j)
+    for j in (2, 1):
+        for n in (2, 3):
+            send(n, j)
+    g2[part] = g2_out[part]
+    wait_all(c2, PARTS)
+    g3[layer] = choose(gid_part, [g2[t] for t in range(PARTS)])
+    start_all(c3, LAYERS)
+
+    for n in range(2):
+        own_copy(n).wait()
+        for j in (1, 3, 2):
+            incoming(n, j).wait_recv()
     to_right.start()
     to_left.start()
-
-    def choose(code, options):
-        code = jnp.full((1, two), code, jnp.int32)
-        total = None
-        for n, option in enumerate(options):
-            option = option.astype(F32)
-            term = jnp.where(code == n, option, jnp.zeros_like(option))
-            total = term if total is None else total + term
-        return total.astype(BF)
-
-    for m in range(GLOBAL):
-        gid = gid_ref[m]
-        cand[m * BLOCK : (m + 1) * BLOCK, :] = choose(
-            lax.div(gid, 2 * GROUPS) * 2 + lax.rem(gid, 2),
-            [kv_own[s, b * BLOCK : (b + 1) * BLOCK, :] for s in range(PARTS) for b in range(2)],
-        )
-
-    def rows(t):
-        return pl.ds(pl.multiple_of(t * 16, 16), 16)
-
-    my_gid = gid_ref[lax.div(spot, PLANE // GLOBAL)]
-    gid_spot = lax.rem(lax.div(my_gid, 2), PLANE)
-    gid_layer = lax.rem(lax.div(my_gid, 2 * PLANE), LAYERS)
-
-    def scatter_plane(source, slots, base):
-        def copy(o):
-            to = lax.rem(spot + o, PLANE)
-            return remote(
-                source.at[rows(to)], slots.at[spot], g_send.at[base, o], g_recv.at[base, o],
-                in_plane(to),
-            )
-        return copy
-
-    def spread_layers(slots, base):
-        def copy(o):
-            to = lax.rem(layer + o, LAYERS)
-            return remote(
-                slots.at[layer], slots.at[layer], g_send.at[base, o], g_recv.at[base, o],
-                in_layer(to),
-            )
-        return copy
-
-    def gather_plane(whole, base):
-        def copy(o):
-            to = lax.rem(spot + o, PLANE)
-            return remote(
-                whole.at[rows(spot)], whole.at[rows(spot)], g_send.at[base, o],
-                g_recv.at[base, o], in_plane(to),
-            )
-        return copy
-
-    def start_all(copy, count):
-        def step(o, _):
-            copy(o).start()
-            return 0
-        lax.fori_loop(1, count, step, 0)
-
-    def wait_all(copy, count):
-        def step(o, _):
-            copy(o).wait()
-            return 0
-        lax.fori_loop(1, count, step, 0)
-
-    c1 = scatter_plane(cand, g1, 0)
-    start_all(c1, PLANE)
-    g1[spot] = cand[rows(spot), :]
-    wait_all(c1, PLANE)
-    g2[layer] = choose(gid_spot, [g1[t] for t in range(PLANE)])
-    c2 = spread_layers(g2, 1)
-    start_all(c2, LAYERS)
-    wait_all(c2, LAYERS)
-    kv_glob[rows(spot), :] = choose(gid_layer, [g2[t] for t in range(LAYERS)])
-    c3 = gather_plane(kv_glob, 2)
-    start_all(c3, PLANE)
-    wait_all(c3, PLANE)
-
+    for j in (3,):
+        for n in (2, 3):
+            send(n, j)
+    wait_all(c3, LAYERS)
+    kv_glob[rows(spot), :] = choose(gid_layer, [g3[t] for t in range(LAYERS)])
+    start_all(c4, PLANE)
+    wait_all(c4, PLANE)
     to_right.wait()
     to_left.wait()
 
@@ -219,7 +231,7 @@
         return pltpu.make_async_copy(dq_stage.at[part], dq_out.at[:, cols(part)], dq_recv.at[0])
 
     def visit(t, _):
-        j = t + t // 2 - 2 * (t // 3)
+        j = t + (t == 1).astype(jnp.int32) - (t == 2).astype(jnp.int32)
         here = lax.rem(part + PARTS - j, PARTS)
         for n in (2, 3):
             @pl.when(j == 0)
@@ -301,79 +313,84 @@
                 add(near_entry, part_grad - far_grad)
                 add(far_entry, far_grad)
 
-        @pl.when(j == 0)
-        def _():
-            own_dq().start()
-
-        @pl.when(j != 0)
-        def _():
-            outgoing_dq(PARTS - j).start()
-
         return 0
 
     lax.fori_loop(0, PARTS, visit, 0)
 
-    c4 = scatter_plane(acc_glob, h1, 3)
-    start_all(c4, PLANE)
+    d1 = around(4, PLANE, spot, in_plane, lambda to: h1_out.at[to], lambda i: h1.at[i])
+    d2 = around(5, LAYERS, layer, in_layer, lambda to: h2.at[layer], lambda i: h2.at[i])
+    d3 = around(6, PLANE, spot, in_plane, lambda to: h3.at[spot], lambda i: h3.at[i])
+
+    for t in range(PLANE):
+        h1_out[t] = acc_glob[t * 16 : (t + 1) * 16, :].astype(BF)
+    start_all(d1, PLANE)
     edge_out[0] = acc_left[...].astype(BF)
     edge_out[1] = acc_right[...].astype(BF)
     back_left = remote(edge_out.at[0], edge_in.at[0], edge_send.at[2], edge_recv.at[2], left)
     back_right = remote(edge_out.at[1], edge_in.at[1], edge_send.at[3], edge_recv.at[3], right)
     back_left.start()
     back_right.start()
-    h1[spot] = acc_glob[rows(spot), :]
-    wait_all(c4, PLANE)
-    h2[layer] = jnp.sum(h1[...], axis=0)
-    c5 = spread_layers(h2, 4)
-    start_all(c5, LAYERS)
-    wait_all(c5, LAYERS)
-    tot_glob[rows(spot), :] = jnp.sum(h2[...], axis=0)
-    c6 = gather_plane(tot_glob, 5)
-    start_all(c6, PLANE)
-
+    own_dq().start()
+    outgoing_dq(2).start()
+    h1[spot] = h1_out[spot]
+    wait_all(d1, PLANE)
+    h2[layer] = jnp.sum(h1[...].astype(F32), axis=0).astype(BF)
+    start_all(d2, LAYERS)
+    outgoing_dq(1).start()
+    outgoing_dq(3).start()
     back_left.wait()
     back_right.wait()
-    acc_own[:, BLOCK : 2 * BLOCK, :] += edge_in[0].astype(F32)
-    acc_own[:, 0:BLOCK, :] += edge_in[1].astype(F32)
-    wait_all(c6, PLANE)
-
-    def outgoing(stage, out, n, j):
+    for b in range(2):
+        acc_own[:, b * BLOCK : (b + 1) * BLOCK, :] += edge_in[1 - b].astype(F32)
+    wait_all(d2, LAYERS)
+    h3[spot] = jnp.sum(h2[...].astype(F32), axis=0).astype(BF)
+    start_all(d3, PLANE)
+    wait_all(d3, PLANE)
+
+    results = ((dk_stage, dk_out), (dv_stage, dv_out))
+
+    def outgoing(n, j):
+        stage, out = results[n]
         to = lax.rem(part + j, PARTS)
         return remote(
             stage.at[to], out.at[:, cols(part)], dkv_send.at[n, j], dkv_recv.at[n, j], mate(to)
         )
 
-    def own_out(stage, out, n):
+    def own_out(n):
+        stage, out = results[n]
         return pltpu.make_async_copy(stage.at[part], out.at[:, cols(part)], dkv_recv.at[n, 0])
 
-    results = ((dk_stage, dk_out), (dv_stage, dv_out))
     for j in (2, 1, 3, 0):
         there = lax.rem(part + j, PARTS)
         for b in range(2):
+            span = slice(b * BLOCK, (b + 1) * BLOCK)
             number = there * (2 * GROUPS) + 2 * group + b
-            total = acc_own[there, b * BLOCK : (b + 1) * BLOCK, :]
+            total = acc_own[there, span, :]
             for m in range(GLOBAL):
-                extra = tot_glob[m * BLOCK : (m + 1) * BLOCK, :]
+                extra = h3[m * 4 : (m + 1) * 4].reshape(BLOCK, two).astype(F32)
                 named = jnp.full((1, two), gid_ref[m], jnp.int32) == number
                 total = total + jnp.where(named, extra, jnp.zeros_like(extra))
-            dk_stage[there, b * BLOCK : (b + 1) * BLOCK, :] = total[:, 0:W].astype(BF)
-            dv_stage[there, b * BLOCK : (b + 1) * BLOCK, :] = total[:, W : 2 * W].astype(BF)
-        for n, (stage, out) in enumerate(results):
+            dk_stage[there, span, :] = total[:, 0:W].astype(BF)
+            dv_stage[there, span, :] = total[:, W:two].astype(BF)
+        for n in range(2):
             if j == 0:
-                own_out(stage, out, n).start()
+                own_out(n).start()
             else:
-                outgoing(stage, out, n, j).start()
-
+                outgoing(n, j).start()
+
+    for copy, count in finish:
+        for o in range(1, count):
+            copy(o).wait_send()
     for n in range(4):
         for j in range(1, PARTS):
             incoming(n, j).wait_send()
     own_dq().wait()
     for j in range(1, PARTS):
         outgoing_dq(j).wait()
-    for n, (stage, out) in enumerate(results):
-        own_out(stage, out, n).wait()
+    for n in range(2):
+        own_out(n).wait()
         for j in range(1, PARTS):
-            outgoing(stage, out, n, j).wait()
+            outgoing(n, j).wait()
 
 
 def on_device(queries, key_vectors, value_vectors, output_grad, rand_pick, global_ids):
@@ -388,8 +405,11 @@
         pltpu.VMEM((PARTS, 2 * BLOCK, two), BF),
         pltpu.VMEM((PARTS, BLOCK, two), BF),
         pltpu.VMEM((PARTS, BLOCK, two), BF),
-        pltpu.VMEM((GLOBAL * BLOCK, two), BF),
-        pltpu.VMEM((PLANE, 16, two), BF),
+        pltpu.VMEM((2, 2 * BLOCK, FULL), BF),
+        pltpu.VMEM((PLANE, 16, 2 * FULL), BF),
+        pltpu.VMEM((PLANE, 16, 2 * FULL), BF),
+        pltpu.VMEM((PARTS, 16, two), BF),
+        pltpu.VMEM((PARTS, 16, two), BF),
         pltpu.VMEM((LAYERS, 16, two), BF),
         pltpu.VMEM((GLOBAL * BLOCK, two), BF),
         pltpu.VMEM((PARTS, 2 * BLOCK, two), F32),
@@ -398,18 +418,20 @@
         pltpu.VMEM((GLOBAL * BLOCK, two), F32),
         pltpu.VMEM((2, PARTS, BLOCK, two), BF),
         pltpu.VMEM((2, PARTS, BLOCK, two), BF),
-        pltpu.VMEM((PLANE, 16, two), F32),
-        pltpu.VMEM((LAYERS, 16, two), F32),
-        pltpu.VMEM((GLOBAL * BLOCK, two), F32),
+        pltpu.VMEM((PLANE, 16, two), BF),
+        pltpu.VMEM((PLANE, 16, two), BF),
+        pltpu.VMEM((LAYERS, 16, two), BF),
+        pltpu.VMEM((PLANE, 16, two), BF),
         pltpu.VMEM((PARTS, 2 * BLOCK, W), BF),
         pltpu.VMEM((PARTS, 2 * BLOCK, W), BF),
         pltpu.VMEM((PARTS, 2 * BLOCK, W), BF),
+        pltpu.SemaphoreType.DMA((2,)),
         pltpu.SemaphoreType.DMA((4, PARTS)),
         pltpu.SemaphoreType.DMA((4, PARTS)),
         pltpu.SemaphoreType.DMA((4,)),
         pltpu.SemaphoreType.DMA((4,)),
-        pltpu.SemaphoreType.DMA((6, PLANE)),
-        pltpu.SemaphoreType.DMA((6, PLANE)),
+        pltpu.SemaphoreType.DMA((8, PLANE)),
+        pltpu.SemaphoreType.DMA((8, PLANE)),
         pltpu.SemaphoreType.DMA((PARTS,)),
         pltpu.SemaphoreType.DMA((PARTS,)),
         pltpu.SemaphoreType.DMA((2, PARTS)),
@@ -422,7 +444,7 @@
         out_specs=(anywhere,) * 3,
         scratch_shapes=scratch,
         compiler_params=pltpu.CompilerParams(
-            collective_id=1, has_side_effects=True, vmem_limit_bytes=32 * 1024 * 1024
+            collective_id=1, has_side_effects=True, vmem_limit_bytes=60 * 1024 * 1024
         ),
         name="sparse_attention_grads",
     )(queries, key_vectors, value_vectors, output_grad, rand_pick.T, global_ids)

time: 88.8 us -> 84.8 us (0.955)
  local copies, waits for them, and re-layouts: 6.92 us -> 3.21 us
    unnamed x15 -> x7, local copies, waits for them, and re-layouts: 6.92 us -> 3.21 us
where the time goes in v2:
time: 84.8 us; the launch traced here: 84.6 us
  Pallas kernels  80.8 us (95%)
  local copies, waits for them, and re-layouts  3.21 us (4%)
    pallas_call x1, Pallas kernels, on_device(): pl.pallas_call(kernel, out_shape=(out, out, out), in_specs=[anywhere] * 4...  80.8 us
    unnamed x7, local copies, waits for them, and re-layouts  3.21 us

profile of v2, /device:TPU:24, one launch (start us, length us, event | category | flops | bytes accessed | tf_op | source)
XLA Modules:
  0.0 84.6 jit_solution(11404476297012562174)
XLA Ops:
  0.6 80.8 %sparse_attention_grads.1 = (bf16[128,512]{1,0:T(8,128)(2,1)}, bf16[128,512]{1,0:T(8,128)(2,1)}, bf16[128,512]{1,0:T(8,128)(2,1)}) custom-call(bf16[128,512]{1,0:T(8,128)(2,1)} %q_hbm.1, bf16[128,512]{1,0:T(8,128)(2,1)} %k_hbm.1, bf16[128,512]{1,0:T(8,128)(2,1)} %v_hbm.1, bf16[128,512]{1,0:T(8,128)(2,1)} %do_hbm.1, s32[3,256]{1,0:T(4,128)} %bitcast.1, s32[2]{0:T(128)} %gid_ref.1), custom_call_target="tpu_custom_call" | custom-call | tf_op jit(solution)/shard_map/sparse_attention_grads/pallas_call | solution.py:440
  81.4 0.0 copy-start.1
  81.4 1.6 %copy.12 = bf16[128,512]{1,0:T(8,128)(2,1)} copy(bf16[128,512]{1,0:T(8,128)(2,1)} %get-tuple-element.6) | data formatting | bytes 262144
  83.0 0.0 copy-done.1
  83.0 0.0 copy-start
  83.0 0.7 copy.13
  83.7 0.3 copy-done
  84.0 0.7 copy.14
Async XLA Ops:
  81.4 1.6 %copy-start.1 = (bf16[128,512]{1,0:T(8,128)(2,1)S(1)}, bf16[128,512]{1,0:T(8,128)(2,1)}, u32[]{:S(2)}) copy-start(bf16[128,512]{1,0:T(8,128)(2,1)} %get-tuple-element.7) | copy-start | bytes 393220
  83.0 1.0 %copy-start = (bf16[128,512]{1,0:T(8,128)(2,1)S(1)}, bf16[128,512]{1,0:T(8,128)(2,1)}, u32[]{:S(2)}) copy-start(bf16[128,512]{1,0:T(8,128)(2,1)} %get-tuple-element.8) | copy-start | bytes 393220

commit v3 on v2

v3 whole, which is shorter than its diff:
```python
import functools

import jax
import jax.numpy as jnp
from jax import lax
from jax.experimental import pallas as pl
from jax.experimental.pallas import tpu as pltpu
from jax.sharding import PartitionSpec as P

MESH = pl.DeviceIdType.MESH
BLOCK = 64
RAND = 3
GLOBAL = 2
PARTS = 4
PLANE = 8
LAYERS = 4
GROUPS = PLANE * LAYERS
SEQ = PARTS * GROUPS
W = 128
HALF = 64
FULL = PARTS * W
BF = jnp.bfloat16
F32 = jnp.float32


def kernel(
    q_hbm, k_hbm, v_hbm, do_hbm, pick_hbm, gid_hbm,
    dq_out, dk_out, dv_out,
    q_all, do_all, kv_own, kv_left, kv_right,
    kv_raw, cand, g1, g2_out, g2, g3, kv_glob,
    acc_own, acc_left, acc_right, acc_glob,
    edge_out, edge_in, h1_out, h1, h2, h3,
    dq_stage, dk_stage, dv_stage,
    keys_near, q2_all, do2_all, expo_near, gp_near, stats, probs_all, grads_all,
    pick_ref, gid_ref, raw_sem, in_send, in_recv, edge_send, edge_recv, g_send, g_recv,
    dq_send, dq_recv, dkv_send, dkv_recv,
):
    me = lax.axis_index("seq")
    part = lax.div(me, GROUPS)
    group = lax.rem(me, GROUPS)
    layer = lax.div(group, PLANE)
    spot = lax.rem(group, PLANE)

    def mate(quarter):
        return {"seq": quarter * GROUPS + group}

    def in_plane(other):
        return {"seq": part * GROUPS + layer * PLANE + other}

    def in_layer(other):
        return {"seq": part * GROUPS + other * PLANE + spot}

    right = {"seq": part * GROUPS + lax.rem(group + 1, GROUPS)}
    left = {"seq": part * GROUPS + lax.rem(group + GROUPS - 1, GROUPS)}

    barrier = pltpu.get_barrier_semaphore()

    def greet(where):
        pl.semaphore_signal(barrier, inc=1, device_id=where, device_id_type=MESH)

    for j in range(1, PARTS):
        greet(mate(lax.rem(part + j, PARTS)))
    greet(left)
    greet(right)
    for o in range(1, PLANE):
        greet(in_plane(lax.rem(spot + o, PLANE)))
    for o in range(1, LAYERS):
        greet(in_layer(lax.rem(layer + o, LAYERS)))
    def remote(src, dst, send, recv, where):
        return pltpu.make_async_remote_copy(
            src_ref=src, dst_ref=dst, send_sem=send, recv_sem=recv, device_id=where,
            device_id_type=MESH,
        )

    two = 2 * W

    def cols(quarter):
        return pl.ds(pl.multiple_of(quarter * W, W), W)

    arrays = (
        (k_hbm, lambda s: kv_own.at[s, :, 0:W]),
        (v_hbm, lambda s: kv_own.at[s, :, W : 2 * W]),
        (q_hbm, lambda s: q_all.at[s]),
        (do_hbm, lambda s: do_all.at[s]),
    )

    def incoming(n, j):
        hbm, place = arrays[n]
        to = lax.rem(part + j, PARTS)
        return remote(
            hbm.at[:, cols(to)], place(part), in_send.at[n, j], in_recv.at[n, j], mate(to)
        )

    def own_copy(n):
        hbm, place = arrays[n]
        return pltpu.make_async_copy(hbm.at[:, cols(part)], place(part), in_recv.at[n, 0])

    def raw_copy(n):
        return pltpu.make_async_copy((k_hbm, v_hbm)[n], kv_raw.at[n], raw_sem.at[n])

    pick_copy = pltpu.make_async_copy(pick_hbm, pick_ref, raw_sem.at[2])
    gid_copy = pltpu.make_async_copy(gid_hbm, gid_ref, raw_sem.at[3])
    gid_copy.start()
    for n in range(2):
        raw_copy(n).start()
    pick_copy.start()
    for n in range(4):
        own_copy(n).start()

    def choose(code, options):
        code = jnp.full((1, options[0].shape[-1]), code, jnp.int32)
        total = None
        for n, option in enumerate(options):
            option = option.astype(F32)
            term = jnp.where(code == n, option, jnp.zeros_like(option))
            total = term if total is None else total + term
        return total.astype(BF)

    def rows(t):
        return pl.ds(pl.multiple_of(t * 16, 16), 16)

    def around(base, count, here, where, source, place):
        def copy(o):
            to = lax.rem(here + o, count)
            return remote(
                source(to), place(here), g_send.at[base, o], g_recv.at[base, o], where(to)
            )
        return copy

    finish = []

    def start_all(copy, count):
        for o in range(1, count):
            copy(o).start()

    def wait_all(copy, count):
        for o in range(1, count):
            copy(o).wait_recv()
        finish.append((copy, count))

    c1 = around(0, PLANE, spot, in_plane, lambda to: cand.at[to], lambda i: g1.at[i])
    c2 = around(1, PARTS, part, mate, lambda to: g2_out.at[to], lambda i: g2.at[i])
    c3 = around(2, LAYERS, layer, in_layer, lambda to: g3.at[layer], lambda i: g3.at[i])
    c4 = around(
        3, PLANE, spot, in_plane, lambda to: kv_glob.at[rows(spot)], lambda i: kv_glob.at[rows(i)]
    )

    to_right = remote(
        kv_own.at[:, BLOCK : 2 * BLOCK, :], kv_left, edge_send.at[0], edge_recv.at[0], right
    )
    to_left = remote(
        kv_own.at[:, 0:BLOCK, :], kv_right, edge_send.at[1], edge_recv.at[1], left
    )

    pl.semaphore_wait(barrier, PARTS - 1 + 2 + PLANE - 1 + LAYERS - 1)


    def send(n, j):
        incoming(n, j).start()

    send(0, 2)
    gid_copy.wait()
    pick_copy.wait()
    my_gid = gid_ref[lax.div(spot, PLANE // GLOBAL)]
    gid_spot = lax.rem(lax.div(my_gid, 2), PLANE)
    gid_layer = lax.rem(lax.div(my_gid, 2 * PLANE), LAYERS)
    gid_part = lax.div(my_gid, 2 * GROUPS)
    for n in range(2):
        raw_copy(n).wait()
    for t in range(PLANE):
        odd = lax.rem(gid_ref[t // (PLANE // GLOBAL)], 2)
        start = (t % (PLANE // GLOBAL)) * 16
        for n in range(2):
            cand[t, :, n * FULL : (n + 1) * FULL] = choose(
                odd, [kv_raw[n, b * BLOCK + start : b * BLOCK + start + 16, :] for b in range(2)]
            )

    start_all(c1, PLANE)
    send(0, 1)
    send(0, 3)
    g1[spot] = cand[spot]
    wait_all(c1, PLANE)
    piece = choose(gid_spot, [g1[t] for t in range(PLANE)])
    for h in range(PARTS):
        g2_out[h, :, 0:W] = piece[:, h * W : (h + 1) * W]
        g2_out[h, :, W:two] = piece[:, FULL + h * W : FULL + (h + 1) * W]
    start_all(c2, PARTS)
    send(1, 2)
    send(1, 1)
    send(1, 3)
    send(2, 2)
    send(3, 2)
    send(2, 1)
    send(3, 1)
    g2[part] = g2_out[part]
    acc_own[...] = jnp.zeros_like(acc_own)
    acc_left[...] = jnp.zeros_like(acc_left)
    acc_right[...] = jnp.zeros_like(acc_right)
    acc_glob[...] = jnp.zeros_like(acc_glob)
    wait_all(c2, PARTS)
    g3[layer] = choose(gid_part, [g2[t] for t in range(PARTS)])
    start_all(c3, LAYERS)
    send(2, 3)
    send(3, 3)

    for n in range(2):
        own_copy(n).wait()
        for j in (1, 3, 2):
            incoming(n, j).wait_recv()
    to_right.start()
    to_left.start()
    wait_all(c3, LAYERS)
    kv_glob[rows(spot), :] = choose(gid_layer, [g3[t] for t in range(LAYERS)])
    start_all(c4, PLANE)
    first_group = (group == 0).astype(jnp.int32)
    last_group = (group == GROUPS - 1).astype(jnp.int32)
    low = lax.broadcasted_iota(jnp.int32, (BLOCK, W), 1) < HALF

    def two_heads(x):
        x = x.astype(F32)
        zero = jnp.zeros_like(x)
        return jnp.concatenate([jnp.where(low, x, zero), jnp.where(low, zero, x)], axis=0)

    def dot(a, b, dims):
        return lax.dot_general(a, b, (dims, ((), ())), preferred_element_type=F32)

    near = (3 + RAND) * BLOCK

    def quarter_of(t):
        j = t + (t == 1).astype(jnp.int32) - (t == 2).astype(jnp.int32)
        return j, lax.rem(part + PARTS - j, PARTS)

    def entries(here, b):
        at_left = lax.rem(here + (PARTS - 1) * first_group, PARTS)
        at_right = lax.rem(here + last_group, PARTS)
        number = here * (2 * GROUPS) + 2 * group + b
        own0 = (kv_own, here, 0, acc_own)
        own1 = (kv_own, here, BLOCK, acc_own)
        window = [
            (kv_left, at_left, 0, acc_left) if b == 0 else own0,
            own0 if b == 0 else own1,
            own1 if b == 0 else (kv_right, at_right, 0, acc_right),
        ]
        choices = []
        for s in range(RAND):
            far = lax.rem(here + PARTS - (s + 1), PARTS)
            far_left = lax.rem(far + (PARTS - 1) * first_group, PARTS)
            pick = jnp.full((1, two), pick_ref[s, number].astype(F32)).astype(BF)
            near_entry = (kv_own, far, b * BLOCK, acc_own)
            far_entry = (kv_left, far_left, 0, acc_left) if b == 0 else (kv_own, far, 0, acc_own)
            choices.append((near_entry, far_entry, pick))
        return number, window, choices

    def load(entry):
        ref, at, start, _ = entry
        return ref[at, start : start + BLOCK, :]

    def add(entry, value):
        _, at, start, acc = entry
        acc[at, start : start + BLOCK, :] += value

    def own_part(t, _):
        j, here = quarter_of(t)
        for n in (2, 3):
            @pl.when(j == 0)
            def _():
                own_copy(n).wait()

            @pl.when(j != 0)
            def _():
                incoming(n, j).wait_recv()

        for b in range(2):
            at = 2 * t + b
            number, window, choices = entries(here, b)
            pieces = [load(e) for e in window]
            for near_entry, far_entry, pick in choices:
                pieces.append(load(near_entry) * (1 - pick) + load(far_entry) * pick)
            listed = jnp.concatenate(pieces, axis=0)
            keys = listed[:, 0:W]
            values = listed[:, W:two]
            q2 = (two_heads(q_all[here, b * BLOCK : (b + 1) * BLOCK, :]) * 0.125).astype(BF)
            do2 = two_heads(do_all[here, b * BLOCK : (b + 1) * BLOCK, :]).astype(BF)
            scores = dot(keys, q2, ((1,), (1,)))
            edge = 0 if b == 0 else 2
            outside = number == (0 if b == 0 else 2 * SEQ - 1)
            masked = jnp.where(outside, -1e30, scores[edge * BLOCK : (edge + 1) * BLOCK])
            ahead = [scores[: edge * BLOCK]] if b else []
            scores = jnp.concatenate(ahead + [masked, scores[(edge + 1) * BLOCK :]], axis=0)
            row_max = jnp.max(scores, axis=0, keepdims=True)
            expo = jnp.exp(scores - row_max)
            keys_near[at] = keys
            q2_all[at] = q2
            do2_all[at] = do2
            expo_near[at] = expo
            gp_near[at] = dot(values, do2, ((1,), (1,)))
            stats[at, 0:1, :] = row_max
            stats[at, 1:2, :] = jnp.sum(expo, axis=0, keepdims=True)
        return 0

    def whole_rows(t, _):
        keys = kv_glob[:, 0:W]
        values = kv_glob[:, W:two]
        for b in range(2):
            at = 2 * t + b
            q2 = q2_all[at]
            do2 = do2_all[at]
            scores = dot(keys, q2, ((1,), (1,)))
            grad_probs = dot(values, do2, ((1,), (1,)))
            near_max = stats[at, 0:1, :]
            row_max = jnp.maximum(near_max, jnp.max(scores, axis=0, keepdims=True))
            shrink = jnp.exp(near_max - row_max)
            expo = jnp.exp(scores - row_max)
            row_total = stats[at, 1:2, :] * shrink + jnp.sum(expo, axis=0, keepdims=True)
            inverse = 1.0 / row_total
            probs = expo * inverse
            probs_half = probs.astype(BF)
            probs_near = expo_near[at] * (shrink * inverse)
            half_near = probs_near.astype(BF)
            gp = gp_near[at]
            row_dot = jnp.sum(probs_half.astype(F32) * grad_probs, axis=0, keepdims=True) + jnp.sum(
                half_near.astype(F32) * gp, axis=0, keepdims=True
            )
            grad_half = (probs * (grad_probs - row_dot)).astype(BF)
            probs_all[at] = half_near
            grads_all[at, 0:near, :] = (probs_near * (gp - row_dot)).astype(BF)
            grads_all[at, near:, :] = grad_half
            acc_glob[:, 0:W] += dot(grad_half, q2, ((1,), (0,)))
            acc_glob[:, W:two] += dot(probs_half, do2, ((1,), (0,)))
        return 0

    def spread(t, _):
        _, here = quarter_of(t)
        for b in range(2):
            at = 2 * t + b
            _, window, choices = entries(here, b)
            grad_near = grads_all[at, 0:near, :]
            back = dot(grad_near, keys_near[at], ((0,), (0,))) + dot(
                grads_all[at, near:, :], kv_glob[:, 0:W], ((0,), (0,))
            )
            dq_stage[here, b * BLOCK : (b + 1) * BLOCK, :] = (
                jnp.where(low, back[:BLOCK], back[BLOCK:]) * 0.125
            ).astype(BF)
            grads = jnp.concatenate(
                [
                    dot(grad_near, q2_all[at], ((1,), (0,))),
                    dot(probs_all[at], do2_all[at], ((1,), (0,))),
                ],
                axis=1,
            )
            for n, entry in enumerate(window):
                add(entry, grads[n * BLOCK : (n + 1) * BLOCK])
            for n, (near_entry, far_entry, pick) in enumerate(choices):
                part_grad = grads[(3 + n) * BLOCK : (4 + n) * BLOCK]
                far_grad = part_grad * pick.astype(F32)
                add(near_entry, part_grad - far_grad)
                add(far_entry, far_grad)
        return 0

    def outgoing_dq(j):
        to = lax.rem(part + j, PARTS)
        return remote(
            dq_stage.at[to], dq_out.at[:, cols(part)], dq_send.at[j], dq_recv.at[j], mate(to)
        )

    def own_dq():
        return pltpu.make_async_copy(dq_stage.at[part], dq_out.at[:, cols(part)], dq_recv.at[0])

    to_right.wait()
    to_left.wait()
    lax.fori_loop(0, PARTS, own_part, 0)
    wait_all(c4, PLANE)
    lax.fori_loop(0, PARTS, whole_rows, 0)

    d1 = around(4, PLANE, spot, in_plane, lambda to: h1_out.at[to], lambda i: h1.at[i])
    d2 = around(5, LAYERS, layer, in_layer, lambda to: h2.at[layer], lambda i: h2.at[i])
    d3 = around(6, PLANE, spot, in_plane, lambda to: h3.at[spot], lambda i: h3.at[i])

    for t in range(PLANE):
        h1_out[t] = acc_glob[t * 16 : (t + 1) * 16, :].astype(BF)
    start_all(d1, PLANE)
    h1[spot] = h1_out[spot]
    lax.fori_loop(0, PARTS, spread, 0)
    own_dq().start()
    wait_all(d1, PLANE)
    h2[layer] = jnp.sum(h1[...].astype(F32), axis=0).astype(BF)
    start_all(d2, LAYERS)
    edge_out[0] = acc_left[...].astype(BF)
    edge_out[1] = acc_right[...].astype(BF)
    back_left = remote(edge_out.at[0], edge_in.at[0], edge_send.at[2], edge_recv.at[2], left)
    back_right = remote(edge_out.at[1], edge_in.at[1], edge_send.at[3], edge_recv.at[3], right)
    back_left.start()
    back_right.start()
    wait_all(d2, LAYERS)
    h3[spot] = jnp.sum(h2[...].astype(F32), axis=0).astype(BF)
    start_all(d3, PLANE)
    outgoing_dq(2).start()
    outgoing_dq(1).start()
    outgoing_dq(3).start()
    back_left.wait()
    back_right.wait()
    for b in range(2):
        acc_own[:, b * BLOCK : (b + 1) * BLOCK, :] += edge_in[1 - b].astype(F32)
    wait_all(d3, PLANE)

    results = ((dk_stage, dk_out), (dv_stage, dv_out))

    def outgoing(n, j):
        stage, out = results[n]
        to = lax.rem(part + j, PARTS)
        return remote(
            stage.at[to], out.at[:, cols(part)], dkv_send.at[n, j], dkv_recv.at[n, j], mate(to)
        )

    def own_out(n):
        stage, out = results[n]
        return pltpu.make_async_copy(stage.at[part], out.at[:, cols(part)], dkv_recv.at[n, 0])

    for j in (2, 1, 3, 0):
        there = lax.rem(part + j, PARTS)
        for b in range(2):
            span = slice(b * BLOCK, (b + 1) * BLOCK)
            number = there * (2 * GROUPS) + 2 * group + b
            total = acc_own[there, span, :]
            for m in range(GLOBAL):
                extra = h3[m * 4 : (m + 1) * 4].reshape(BLOCK, two).astype(F32)
                named = jnp.full((1, two), gid_ref[m], jnp.int32) == number
                total = total + jnp.where(named, extra, jnp.zeros_like(extra))
            dk_stage[there, span, :] = total[:, 0:W].astype(BF)
            dv_stage[there, span, :] = total[:, W:two].astype(BF)
        for n in range(2):
            if j == 0:
                own_out(n).start()
            else:
                outgoing(n, j).start()

    for copy, count in finish:
        for o in range(1, count):
            copy(o).wait_send()
    for n in range(4):
        for j in range(1, PARTS):
            incoming(n, j).wait_send()
    own_dq().wait()
    for j in range(1, PARTS):
        outgoing_dq(j).wait()
    for n in range(2):
        own_out(n).wait()
        for j in range(1, PARTS):
            outgoing(n, j).wait()


def on_device(queries, key_vectors, value_vectors, output_grad, rand_pick, global_ids):
    rows, width = queries.shape
    out = jax.ShapeDtypeStruct((rows, width), BF)
    anywhere = pl.BlockSpec(memory_space=pl.ANY)
    two = 2 * W
    scratch = [
        pltpu.VMEM((PARTS, 2 * BLOCK, W), BF),
        pltpu.VMEM((PARTS, 2 * BLOCK, W), BF),
        pltpu.VMEM((PARTS, 2 * BLOCK, two), BF),
        pltpu.VMEM((PARTS, BLOCK, two), BF),
        pltpu.VMEM((PARTS, BLOCK, two), BF),
        pltpu.VMEM((2, 2 * BLOCK, FULL), BF),
        pltpu.VMEM((PLANE, 16, 2 * FULL), BF),
        pltpu.VMEM((PLANE, 16, 2 * FULL), BF),
        pltpu.VMEM((PARTS, 16, two), BF),
        pltpu.VMEM((PARTS, 16, two), BF),
        pltpu.VMEM((LAYERS, 16, two), BF),
        pltpu.VMEM((GLOBAL * BLOCK, two), BF),
        pltpu.VMEM((PARTS, 2 * BLOCK, two), F32),
        pltpu.VMEM((PARTS, BLOCK, two), F32),
        pltpu.VMEM((PARTS, BLOCK, two), F32),
        pltpu.VMEM((GLOBAL * BLOCK, two), F32),
        pltpu.VMEM((2, PARTS, BLOCK, two), BF),
        pltpu.VMEM((2, PARTS, BLOCK, two), BF),
        pltpu.VMEM((PLANE, 16, two), BF),
        pltpu.VMEM((PLANE, 16, two), BF),
        pltpu.VMEM((LAYERS, 16, two), BF),
        pltpu.VMEM((PLANE, 16, two), BF),
        pltpu.VMEM((PARTS, 2 * BLOCK, W), BF),
        pltpu.VMEM((PARTS, 2 * BLOCK, W), BF),
        pltpu.VMEM((PARTS, 2 * BLOCK, W), BF),
        pltpu.VMEM((2 * PARTS, 6 * BLOCK, W), BF),
        pltpu.VMEM((2 * PARTS, 2 * BLOCK, W), BF),
        pltpu.VMEM((2 * PARTS, 2 * BLOCK, W), BF),
        pltpu.VMEM((2 * PARTS, 6 * BLOCK, W), F32),
        pltpu.VMEM((2 * PARTS, 6 * BLOCK, W), F32),
        pltpu.VMEM((2 * PARTS, 8, W), F32),
        pltpu.VMEM((2 * PARTS, 6 * BLOCK, W), BF),
        pltpu.VMEM((2 * PARTS, 8 * BLOCK, W), BF),
        pltpu.SMEM((RAND, 2 * SEQ), jnp.int32),
        pltpu.SMEM((GLOBAL,), jnp.int32),
        pltpu.SemaphoreType.DMA((4,)),
        pltpu.SemaphoreType.DMA((4, PARTS)),
        pltpu.SemaphoreType.DMA((4, PARTS)),
        pltpu.SemaphoreType.DMA((4,)),
        pltpu.SemaphoreType.DMA((4,)),
        pltpu.SemaphoreType.DMA((8, PLANE)),
        pltpu.SemaphoreType.DMA((8, PLANE)),
        pltpu.SemaphoreType.DMA((PARTS,)),
        pltpu.SemaphoreType.DMA((PARTS,)),
        pltpu.SemaphoreType.DMA((2, PARTS)),
        pltpu.SemaphoreType.DMA((2, PARTS)),
    ]
    return pl.pallas_call(
        kernel,
        out_shape=(out, out, out),
        in_specs=[anywhere] * 6,
        out_specs=(anywhere,) * 3,
        scratch_shapes=scratch,
        compiler_params=pltpu.CompilerParams(
            collective_id=1, has_side_effects=True, vmem_limit_bytes=60 * 1024 * 1024
        ),
        name="sparse_attention_grads",
    )(queries, key_vectors, value_vectors, output_grad, rand_pick.T, global_ids)


def solution(mesh):
    spec = P(("doc", "seq"), None)
    return jax.shard_map(
        on_device,
        mesh=mesh,
        in_specs=(spec, spec, spec, spec, P("doc", None), P("doc")),
        out_specs=(spec, spec, spec),
        check_vma=False,
    )
```

time: 84.8 us -> 83.3 us (0.982)
  Pallas kernels: 80.8 us -> 78.4 us
    pallas_call x1, Pallas kernels: 80.8 us -> 78.4 us  [on_device(): pl.pallas_call(kernel, out_shape=(out, out, out), in_specs=[anywhere] * 6...]
where the time goes in v3:
time: 83.3 us; the launch traced here: 82.3 us
  Pallas kernels  78.4 us (94%)
  local copies, waits for them, and re-layouts  3.21 us (4%)
    pallas_call x1, Pallas kernels, on_device(): pl.pallas_call(kernel, out_shape=(out, out, out), in_specs=[anywhere] * 6...  78.4 us
    unnamed x7, local copies, waits for them, and re-layouts  3.21 us

profile of v3, /device:TPU:24, one launch (start us, length us, event | category | flops | bytes accessed | tf_op | source)
XLA Modules:
  0.0 82.3 jit_solution(3902634883423443071)
XLA Ops:
  0.6 78.4 %sparse_attention_grads.1 = (bf16[128,512]{1,0:T(8,128)(2,1)}, bf16[128,512]{1,0:T(8,128)(2,1)}, bf16[128,512]{1,0:T(8,128)(2,1)}) custom-call(bf16[128,512]{1,0:T(8,128)(2,1)} %q_hbm.1, bf16[128,512]{1,0:T(8,128)(2,1)} %k_hbm.1, bf16[128,512]{1,0:T(8,128)(2,1)} %v_hbm.1, bf16[128,512]{1,0:T(8,128)(2,1)} %do_hbm.1, s32[3,256]{1,0:T(4,128)} %bitcast.1, s32[2]{0:T(128)} %gid_hbm.1), custom_call_target="tpu_custom_call" | custom-call | tf_op jit(solution)/shard_map/sparse_attention_grads/pallas_call | solution.py:505
  79.1 0.0 copy-start.1
  79.1 1.6 %copy.12 = bf16[128,512]{1,0:T(8,128)(2,1)} copy(bf16[128,512]{1,0:T(8,128)(2,1)} %get-tuple-element.6) | data formatting | bytes 262144
  80.7 0.0 copy-done.1
  80.7 0.0 copy-start
  80.7 0.7 copy.13
  81.3 0.3 copy-done
  81.6 0.7 copy.14
Async XLA Ops:
  79.1 1.6 %copy-start.1 = (bf16[128,512]{1,0:T(8,128)(2,1)S(1)}, bf16[128,512]{1,0:T(8,128)(2,1)}, u32[]{:S(2)}) copy-start(bf16[128,512]{1,0:T(8,128)(2,1)} %get-tuple-element.7) | copy-start | bytes 393220
  80.7 1.0 %copy-start = (bf16[128,512]{1,0:T(8,128)(2,1)S(1)}, bf16[128,512]{1,0:T(8,128)(2,1)}, u32[]{:S(2)}) copy-start(bf16[128,512]{1,0:T(8,128)(2,1)} %get-tuple-element.8) | copy-start | bytes 393220

commit v4 on v3

--- a/solution.py
+++ b/solution.py
@@ -25,7 +25,7 @@
 
 def kernel(
     q_hbm, k_hbm, v_hbm, do_hbm, pick_hbm, gid_hbm,
-    dq_out, dk_out, dv_out,
+    grads_out,
     q_all, do_all, kv_own, kv_left, kv_right,
     kv_raw, cand, g1, g2_out, g2, g3, kv_glob,
     acc_own, acc_left, acc_right, acc_glob,
@@ -36,6 +36,7 @@
     dq_send, dq_recv, dkv_send, dkv_recv,
 ):
     me = lax.axis_index("seq")
+    dq_out, dk_out, dv_out = (grads_out.at[n] for n in range(3))
     part = lax.div(me, GROUPS)
     group = lax.rem(me, GROUPS)
     layer = lax.div(group, PLANE)
@@ -192,6 +193,7 @@
     send(3, 2)
     send(2, 1)
     send(3, 1)
+    send(2, 3)
     g2[part] = g2_out[part]
     acc_own[...] = jnp.zeros_like(acc_own)
     acc_left[...] = jnp.zeros_like(acc_left)
@@ -200,7 +202,6 @@
     wait_all(c2, PARTS)
     g3[layer] = choose(gid_part, [g2[t] for t in range(PARTS)])
     start_all(c3, LAYERS)
-    send(2, 3)
     send(3, 3)
 
     for n in range(2):
@@ -370,7 +371,7 @@
     to_left.wait()
     lax.fori_loop(0, PARTS, own_part, 0)
     wait_all(c4, PLANE)
-    lax.fori_loop(0, PARTS, whole_rows, 0)
+    lax.fori_loop(0, PARTS, whole_rows, 0, unroll=True)
 
     d1 = around(4, PLANE, spot, in_plane, lambda to: h1_out.at[to], lambda i: h1.at[i])
     d2 = around(5, LAYERS, layer, in_layer, lambda to: h2.at[layer], lambda i: h2.at[i])
@@ -451,7 +452,7 @@
 
 def on_device(queries, key_vectors, value_vectors, output_grad, rand_pick, global_ids):
     rows, width = queries.shape
-    out = jax.ShapeDtypeStruct((rows, width), BF)
+    out = jax.ShapeDtypeStruct((3, rows, width), BF)
     anywhere = pl.BlockSpec(memory_space=pl.ANY)
     two = 2 * W
     scratch = [
@@ -502,17 +503,18 @@
         pltpu.SemaphoreType.DMA((2, PARTS)),
         pltpu.SemaphoreType.DMA((2, PARTS)),
     ]
-    return pl.pallas_call(
+    grads = pl.pallas_call(
         kernel,
-        out_shape=(out, out, out),
+        out_shape=out,
         in_specs=[anywhere] * 6,
-        out_specs=(anywhere,) * 3,
+        out_specs=anywhere,
         scratch_shapes=scratch,
         compiler_params=pltpu.CompilerParams(
             collective_id=1, has_side_effects=True, vmem_limit_bytes=60 * 1024 * 1024
         ),
         name="sparse_attention_grads",
     )(queries, key_vectors, value_vectors, output_grad, rand_pick.T, global_ids)
+    return grads[0], grads[1], grads[2]
 
 
 def solution(mesh):

time: 83.3 us -> 80.8 us (0.970)
  local copies, waits for them, and re-layouts: 3.21 us -> 1.78 us
    unnamed x7 -> x0, local copies, waits for them, and re-layouts: 3.21 us -> none
    squeeze x0 -> x1, local copies, waits for them, and re-layouts: none -> 1.78 us  [on_device(): return (grads[0], grads[1], grads[2])]
where the time goes in v4:
time: 80.8 us; the launch traced here: 80.1 us
  Pallas kernels  77.7 us (96%)
  local copies, waits for them, and re-layouts  1.78 us (2%)
    pallas_call x1, Pallas kernels, on_device(): pl.pallas_call(kernel, out_shape=out, in_specs=[anywhere] * 6, out_specs=...  77.7 us
    squeeze x1, local copies, waits for them, and re-layouts, on_device(): return (grads[0], grads[1], grads[2])  1.78 us

profile of v4, /device:TPU:24, one launch (start us, length us, event | category | flops | bytes accessed | tf_op | source)
XLA Modules:
  0.0 80.1 jit_solution(6643901405605343102)
XLA Ops:
  0.6 77.7 %sparse_attention_grads.1 = bf16[3,128,512]{2,1,0:T(8,128)(2,1)} custom-call(bf16[128,512]{1,0:T(8,128)(2,1)} %q_hbm.1, bf16[128,512]{1,0:T(8,128)(2,1)} %k_hbm.1, bf16[128,512]{1,0:T(8,128)(2,1)} %v_hbm.1, bf16[128,512]{1,0:T(8,128)(2,1)} %do_hbm.1, s32[3,256]{1,0:T(4,128)} %bitcast.7, s32[2]{0:T(128)} %gid_hbm.1), custom_call_target="tpu_custom_call" | custom-call | tf_op jit(solution)/shard_map/sparse_attention_grads/pallas_call | solution.py:506
  78.3 1.8 %slice_bitcast_fusion = (bf16[128,512]{1,0:T(8,128)(2,1)}, bf16[128,512]{1,0:T(8,128)(2,1)}, bf16[128,512]{1,0:T(8,128)(2,1)}) fusion(bf16[3,128,512]{2,1,0:T(8,128)(2,1)} %sparse_attention_grads.1), kind=kLoop, calls=%fused_computation | loop fusion | bytes 786432 | tf_op jit(solution)/shard_map/squeeze | solution.py:517

commit v5 on v4

--- a/solution.py
+++ b/solution.py
@@ -28,10 +28,11 @@
     grads_out,
     q_all, do_all, kv_own, kv_left, kv_right,
     kv_raw, cand, g1, g2_out, g2, g3, kv_glob,
-    acc_own, acc_left, acc_right, acc_glob,
+    acc_own, acc_left, acc_right,
     edge_out, edge_in, h1_out, h1, h2, h3,
     dq_stage, dk_stage, dv_stage,
     keys_near, q2_all, do2_all, expo_near, gp_near, stats, probs_all, grads_all,
+    probs_glob, grads_glob,
     pick_ref, gid_ref, raw_sem, in_send, in_recv, edge_send, edge_recv, g_send, g_recv,
     dq_send, dq_recv, dkv_send, dkv_recv,
 ):
@@ -198,7 +199,6 @@
     acc_own[...] = jnp.zeros_like(acc_own)
     acc_left[...] = jnp.zeros_like(acc_left)
     acc_right[...] = jnp.zeros_like(acc_right)
-    acc_glob[...] = jnp.zeros_like(acc_glob)
     wait_all(c2, PARTS)
     g3[layer] = choose(gid_part, [g2[t] for t in range(PARTS)])
     start_all(c3, LAYERS)
@@ -224,8 +224,6 @@
 
     def dot(a, b, dims):
         return lax.dot_general(a, b, (dims, ((), ())), preferred_element_type=F32)
-
-    near = (3 + RAND) * BLOCK
 
     def quarter_of(t):
         j = t + (t == 1).astype(jnp.int32) - (t == 2).astype(jnp.int32)
@@ -324,10 +322,9 @@
             )
             grad_half = (probs * (grad_probs - row_dot)).astype(BF)
             probs_all[at] = half_near
-            grads_all[at, 0:near, :] = (probs_near * (gp - row_dot)).astype(BF)
-            grads_all[at, near:, :] = grad_half
-            acc_glob[:, 0:W] += dot(grad_half, q2, ((1,), (0,)))
-            acc_glob[:, W:two] += dot(probs_half, do2, ((1,), (0,)))
+            grads_all[at] = (probs_near * (gp - row_dot)).astype(BF)
+            grads_glob[:, cols(at)] = grad_half
+            probs_glob[:, cols(at)] = probs_half
         return 0
 
     def spread(t, _):
@@ -335,9 +332,9 @@
         for b in range(2):
             at = 2 * t + b
             _, window, choices = entries(here, b)
-            grad_near = grads_all[at, 0:near, :]
+            grad_near = grads_all[at]
             back = dot(grad_near, keys_near[at], ((0,), (0,))) + dot(
-                grads_all[at, near:, :], kv_glob[:, 0:W], ((0,), (0,))
+                grads_glob[:, cols(at)], kv_glob[:, 0:W], ((0,), (0,))
             )
             dq_stage[here, b * BLOCK : (b + 1) * BLOCK, :] = (
                 jnp.where(low, back[:BLOCK], back[BLOCK:]) * 0.125
@@ -377,8 +374,13 @@
     d2 = around(5, LAYERS, layer, in_layer, lambda to: h2.at[layer], lambda i: h2.at[i])
     d3 = around(6, PLANE, spot, in_plane, lambda to: h3.at[spot], lambda i: h3.at[i])
 
-    for t in range(PLANE):
-        h1_out[t] = acc_glob[t * 16 : (t + 1) * 16, :].astype(BF)
+    sums = (
+        dot(grads_glob[...], q2_all[...].reshape(2 * PARTS * W, W), ((1,), (0,))),
+        dot(probs_glob[...], do2_all[...].reshape(2 * PARTS * W, W), ((1,), (0,))),
+    )
+    for n in range(2):
+        for t in range(PLANE):
+            h1_out[t, :, n * W : (n + 1) * W] = sums[n][t * 16 : (t + 1) * 16].astype(BF)
     start_all(d1, PLANE)
     h1[spot] = h1_out[spot]
     lax.fori_loop(0, PARTS, spread, 0)
@@ -471,7 +473,6 @@
         pltpu.VMEM((PARTS, 2 * BLOCK, two), F32),
         pltpu.VMEM((PARTS, BLOCK, two), F32),
         pltpu.VMEM((PARTS, BLOCK, two), F32),
-        pltpu.VMEM((GLOBAL * BLOCK, two), F32),
         pltpu.VMEM((2, PARTS, BLOCK, two), BF),
         pltpu.VMEM((2, PARTS, BLOCK, two), BF),
         pltpu.VMEM((PLANE, 16, two), BF),
@@ -488,7 +489,9 @@
         pltpu.VMEM((2 * PARTS, 6 * BLOCK, W), F32),
         pltpu.VMEM((2 * PARTS, 8, W), F32),
         pltpu.VMEM((2 * PARTS, 6 * BLOCK, W), BF),
-        pltpu.VMEM((2 * PARTS, 8 * BLOCK, W), BF),
+        pltpu.VMEM((2 * PARTS, 6 * BLOCK, W), BF),
+        pltpu.VMEM((GLOBAL * BLOCK, 2 * PARTS * W), BF),
+        pltpu.VMEM((GLOBAL * BLOCK, 2 * PARTS * W), BF),
         pltpu.SMEM((RAND, 2 * SEQ), jnp.int32),
         pltpu.SMEM((GLOBAL,), jnp.int32),
         pltpu.SemaphoreType.DMA((4,)),

time: 80.8 us -> 79.5 us (0.984)
  Pallas kernels: 77.7 us -> 76.4 us
    pallas_call x1, Pallas kernels: 77.7 us -> 76.4 us  [on_device(): pl.pallas_call(kernel, out_shape=out, in_specs=[anywhere] * 6, out_specs=...]
where the time goes in v5:
time: 79.5 us; the launch traced here: 78.8 us
  Pallas kernels  76.4 us (96%)
  local copies, waits for them, and re-layouts  1.78 us (2%)
    pallas_call x1, Pallas kernels, on_device(): pl.pallas_call(kernel, out_shape=out, in_specs=[anywhere] * 6, out_specs=...  76.4 us
    squeeze x1, local copies, waits for them, and re-layouts, on_device(): return (grads[0], grads[1], grads[2])  1.78 us

profile of v5, /device:TPU:24, one launch (start us, length us, event | category | flops | bytes accessed | tf_op | source)
XLA Modules:
  0.0 78.8 jit_solution(13401780072450094502)
XLA Ops:
  0.6 76.4 %sparse_attention_grads.1 = bf16[3,128,512]{2,1,0:T(8,128)(2,1)} custom-call(bf16[128,512]{1,0:T(8,128)(2,1)} %q_hbm.1, bf16[128,512]{1,0:T(8,128)(2,1)} %k_hbm.1, bf16[128,512]{1,0:T(8,128)(2,1)} %v_hbm.1, bf16[128,512]{1,0:T(8,128)(2,1)} %do_hbm.1, s32[3,256]{1,0:T(4,128)} %bitcast.7, s32[2]{0:T(128)} %gid_hbm.1), custom_call_target="tpu_custom_call" | custom-call | tf_op jit(solution)/shard_map/sparse_attention_grads/pallas_call | solution.py:509
  77.0 1.8 %slice_bitcast_fusion = (bf16[128,512]{1,0:T(8,128)(2,1)}, bf16[128,512]{1,0:T(8,128)(2,1)}, bf16[128,512]{1,0:T(8,128)(2,1)}) fusion(bf16[3,128,512]{2,1,0:T(8,128)(2,1)} %sparse_attention_grads.1), kind=kLoop, calls=%fused_computation | loop fusion | bytes 786432 | tf_op jit(solution)/shard_map/squeeze | solution.py:520
